TPU v7x, 32 devices: a whole 2x2x4 slice. The times are simulated.
32 devices in a mesh: chan: 8 (over z, y), win: 4 (over x, core).
Axes of the slice: x: 2, y: 2, z: 4, core: 2. Of those that a mesh axis runs over, the one named last changes fastest.
Arguments:
- spectra: bfloat16 [4, 1024, 1536], P('win', 'chan'), may hold values from -120 to 120
- masks: int32 [4, 1024], replicated, may hold values from 0 to 1, as said below
- matching: int32 [2, 8], replicated, may hold values from 0 to 7, as said below
Outputs:
- corr: bfloat16 [2, 1024, 8192], P(None, ('chan', 'win'))
Inputs may be any that keep to these rules, and one draw needn't show every extreme that they name: `masks`: some channels are 0 in every window. `matching`: in round r every block i meets block i XOR s_r, with one s_r for each round, and each bit of 7 is set in exactly one of the two rounds' s_r.
All inputs are finite; a program needn't handle non-finite values.
Results may differ from a plain program's by a relative error of at most 0.014.
Values may be sent and summed in bfloat16 or wider, within the bound.
No kernel may reach another device: no remote copies, remote signals or barrier semaphores. Data moves between devices by JAX's collectives and lax.ppermute only.
A program may use at most 64 MiB of HBM per device.

v0:
```python
import functools
import math

import jax
import jax.numpy as jnp
import numpy as np
from jax import lax
from jax.experimental import pallas as pl
from jax.experimental.pallas import tpu as pltpu
from jax.sharding import PartitionSpec as P

LAGS = 64
ROUNDS = 2
LAG_STEP = 16
BIN_STEP = 256
PARTS = 2
SWITCH_BLOCKS = 8

VMEM = pl.BlockSpec(memory_space=pltpu.VMEM)
SMEM = pl.BlockSpec(memory_space=pltpu.SMEM)
PARAMS = pltpu.CompilerParams(vmem_limit_bytes=24 * 2**20)


def flip(value, axis, bits):
    if bits == 0:
        return value
    return lax.ppermute(value, axis, [(i, i ^ bits) for i in range(lax.axis_size(axis))])


def tables(bin_count):
    phase = np.arange(LAGS)[:, None] * np.arange(bin_count)[None, :] % (2 * bin_count)
    angle = phase.astype(np.float64) * (math.pi / bin_count)
    return np.cos(angle).astype(np.float32), np.sin(angle).astype(np.float32)


def descending_bits(size):
    return [1 << k for k in reversed(range(size.bit_length() - 1))]


def own_rows(values):
    held = {0: values}
    count = values.shape[0]
    for bit in descending_bits(lax.axis_size("win")):
        upper = (lax.axis_index("win") & bit) != 0
        half = held[0].shape[1] // 2
        kept, sent = {}, {}
        for d, rows in held.items():
            low, high = rows[:, :half], rows[:, half:]
            kept[d] = jnp.where(upper, high, low)
            sent[d] = jnp.where(upper, low, high)
        keys = list(held)
        moved = flip(jnp.concatenate([sent[d] for d in keys], axis=0), "win", bit)
        for n, d in enumerate(keys):
            kept[d | bit] = moved[n * count : (n + 1) * count]
        held = kept
    return held


def gather_windows(values):
    held = {0: values}
    for bit in descending_bits(lax.axis_size("win")):
        for d in list(held):
            held[d | bit] = flip(held[d], "win", bit)
    return held


def prepare_kernel(spectra_ref, masks_ref, matching_ref, whole_ref, *refs):
    part_refs, pair_ref = refs[:-1], refs[-1]
    w_count, block, two_bins = spectra_ref.shape
    bins = two_bins // 2
    first = matching_ref[0, 0]
    pair_ref[0] = jnp.minimum(first, first ^ (lax.axis_size("chan") - 1))
    at = pl.ds(pl.multiple_of(lax.axis_index("chan") * block, block), block)
    every = masks_ref[:, at].astype(jnp.float32)
    for q in range(w_count):
        window = lax.axis_index("win") * w_count + q
        chosen = lax.broadcasted_iota(jnp.int32, every.shape, 0) == window
        flags = lax.dot_general(
            every,
            chosen.astype(jnp.float32),
            (((0,), (0,)), ((), ())),
            preferred_element_type=jnp.float32,
        )
        chunk = 32
        for c in range(0, block, chunk):
            values = spectra_ref[q, c : c + chunk, :].astype(jnp.float32)
            mean_square = jnp.mean(values * values, axis=-1, keepdims=True)
            factor = flags[c : c + chunk, :1] * lax.rsqrt(mean_square + 1e-06)
            white = (values * factor).astype(jnp.bfloat16)
            whole_ref[q, c : c + chunk, :] = white
            for n, part_ref in enumerate(part_refs):
                width = part_ref.shape[2] // 2
                for side in range(2):
                    part_ref[q, c : c + chunk, side * width : (side + 1) * width] = white[
                        :, side * bins + n * width : side * bins + (n + 1) * width
                    ]


def prepare(spectra, masks, matching):
    w_count, block, two_bins = spectra.shape
    shape = jax.ShapeDtypeStruct
    part = shape((w_count, block, two_bins // PARTS), jnp.bfloat16)
    outs = pl.pallas_call(
        prepare_kernel,
        out_shape=[shape(spectra.shape, jnp.bfloat16)] + [part] * PARTS + [shape((1,), jnp.int32)],
        in_specs=[VMEM, VMEM, SMEM],
        out_specs=[VMEM] * (1 + PARTS) + [SMEM],
        compiler_params=PARAMS,
    )(spectra, masks, matching)
    return outs[0], outs[1:-1], outs[-1][0]


def correlate_kernel(plan, first, last, *refs):
    refs = list(refs)
    take = lambda count: [refs.pop(0) for _ in range(count)]
    cos_ref, sin_ref = take(2)
    if first:
        masks_ref, matching_ref = take(2)
    else:
        (total_ref,) = take(1)
    if last:
        scale_ref, order_ref = take(2)
    own_refs = take(1 + max(piece[0] for piece in plan))
    left_refs = take(len(plan))
    right_refs = take(len(plan))
    rows, block = own_refs[0].shape[1], left_refs[0].shape[1]
    bins = own_refs[0].shape[2] // 2

    def dot(lhs, rhs):
        return lax.dot_general(
            lhs, rhs, (((1,), (1,)), ((), ())), preferred_element_type=jnp.float32
        )

    if first:
        new_scale_ref, counts_ref = refs[1], refs[2]
        block_id, slot = lax.axis_index("chan"), lax.axis_index("win")
        own_at = pl.ds(pl.multiple_of(block_id * block, block), block)
        own_flags = masks_ref[:, own_at].astype(jnp.float32)
        for r in range(ROUNDS):
            partner = block_id ^ matching_ref[r, 0]
            at = pl.ds(pl.multiple_of(partner * block, block), block)
            counts = lax.dot_general(
                own_flags,
                masks_ref[:, at].astype(jnp.float32),
                (((0,), (0,)), ((), ())),
                preferred_element_type=jnp.float32,
            )
            counts_ref[...] = lax.rsqrt(bins * jnp.maximum(counts, 1.0))
            new_scale_ref[r] = counts_ref[pl.ds(pl.multiple_of(slot * rows, rows), rows), :]
    out_ref = refs[0]
    if last:
        swapped = order_ref[0]
        rounds = [swapped, 1 - swapped]
        scales = [scale_ref[r] for r in rounds]

    def one_step(index, carry):
        step = pl.multiple_of(index * LAG_STEP, LAG_STEP)
        total = None
        for n, (own_at, first_bin, width) in enumerate(plan):
            for q in range(own_refs[0].shape[0]):
                for c in range(0, width, BIN_STEP):
                    size = min(BIN_STEP, width - c)
                    b = first_bin + c
                    real = own_refs[own_at][q, :, b : b + size]
                    imag = own_refs[own_at][q, :, bins + b : bins + b + size]
                    cosine = cos_ref[pl.ds(step, LAG_STEP), b : b + size].astype(jnp.bfloat16)
                    sine = sin_ref[pl.ds(step, LAG_STEP), b : b + size].astype(jnp.bfloat16)
                    turned = [[], []]
                    for t in range(LAG_STEP):
                        cos, sin = cosine[t : t + 1], sine[t : t + 1]
                        turned[0].append(real * cos - imag * sin)
                        turned[1].append(real * sin + imag * cos)
                    for side in range(2):
                        at = side * width + c
                        rhs = jnp.concatenate(
                            [ref[q, :, at : at + size] for ref in (left_refs[n], right_refs[n])],
                            axis=0,
                        )
                        term = dot(jnp.concatenate(turned[side], axis=0), rhs)
                        total = term if total is None else total + term
        at = pl.ds(pl.multiple_of(step * rows, LAG_STEP * rows), LAG_STEP * rows)
        if not first:
            total = total + total_ref[at, :]
        if not last:
            out_ref[at, :] = total
            return carry
        for t in range(LAG_STEP):
            lanes = pl.ds(pl.multiple_of((step + t) * block, block), block)
            for side in range(ROUNDS):
                part = total[t * rows : (t + 1) * rows, side * block : (side + 1) * block]
                out_ref[rounds[side], :, lanes] = (part * scales[side]).astype(jnp.bfloat16)
        return carry

    lax.fori_loop(0, LAGS // LAG_STEP, one_step, 0)


def correlate(state, masks, matching, order, pieces, last):
    first = state is None
    own, plan = [], []
    for rows, first_bin, pair in pieces:
        if not any(rows is seen for seen in own):
            own.append(rows)
        at = next(n for n, seen in enumerate(own) if seen is rows)
        plan.append((at, first_bin, pair[0].shape[2] // 2))
    _, rows, two_bins = own[0].shape
    block = pieces[0][2][0].shape[1]
    cos, sin = tables(two_bins // 2)
    arrays = [jnp.asarray(cos), jnp.asarray(sin)]
    specs = [VMEM] * 2
    if first:
        arrays += [masks, matching]
        specs += [VMEM, SMEM]
    else:
        arrays.append(state[0])
        specs.append(VMEM)
    if last:
        arrays += [state[1], order]
        specs += [VMEM, SMEM]
    others = own + [pair[0] for *_, pair in pieces] + [pair[1] for *_, pair in pieces]
    shape = jax.ShapeDtypeStruct
    running = shape((LAGS * rows, ROUNDS * block), jnp.float32)
    if last:
        outs = [shape((ROUNDS, rows, LAGS * block), jnp.bfloat16)]
    elif first:
        outs = [running, shape((ROUNDS, rows, block), jnp.float32)]
    else:
        outs = [running]
    depth = 2 * sum(own[0].shape[0] * width for _, _, width in plan)
    result = pl.pallas_call(
        functools.partial(correlate_kernel, plan, first, last),
        out_shape=outs,
        in_specs=specs + [VMEM] * len(others),
        out_specs=[VMEM] * len(outs),
        scratch_shapes=[pltpu.VMEM((block, block), jnp.float32)] if first else [],
        compiler_params=PARAMS,
        cost_estimate=pl.CostEstimate(
            flops=2 * LAGS * rows * depth * ROUNDS * block,
            bytes_accessed=depth * (ROUNDS * block + rows) * 2,
            transcendentals=0,
        ),
    )(*arrays, *others)
    if last:
        return result[0]
    return (result[0], result[1] if first else state[1])


def after(values, state):
    return lax.optimization_barrier((values, state))


def combine(masks, matching, order, whole, pairs):
    own = own_rows(whole)
    width = pairs[0][0].shape[2] // 2
    low = [bit for bit in descending_bits(lax.axis_size("win"))][-1]
    high = descending_bits(lax.axis_size("win"))[:-1]
    state = None
    held = {0: pairs}
    for bit in high:
        held |= {
            d | bit: [[flip(side, "win", bit) for side in pair] for pair in held[d]] for d in list(held)
        }
    steps = [(d, n) for d in sorted(held) for n in range(len(pairs))]
    for number, (d, n) in enumerate(steps):
        pair = held[d][n]
        if state is not None:
            pair, state = after(pair, state)
        across = [flip(side, "win", low) for side in pair]
        ahead = number + 1
        if 0 < number and ahead < len(steps) and steps[ahead][0] != 0:
            d_ahead, n_ahead = steps[ahead]
            (held[d_ahead][n_ahead], across), state = after((held[d_ahead][n_ahead], across), state)
        pieces = [(own[d], n * width, pair), (own[d | low], n * width, across)]
        state = correlate(state, masks, matching, order, pieces, ahead == len(steps))
    return state


def shards(spectra, masks, matching):
    blocks = lax.axis_size("chan")
    whole, parts, pair = prepare(spectra, masks, matching)

    if blocks > SWITCH_BLOCKS:
        pairs = [[part, part] for part in parts]
        for bit in range(blocks.bit_length() - 1):
            taken = (matching[0, 0] >> bit) & 1 == 1
            for n, (left, right) in enumerate(pairs):
                moved = flip(jnp.where(taken, left, right), "chan", 1 << bit)
                pairs[n] = [jnp.where(taken, moved, left), jnp.where(taken, right, moved)]
        order = jnp.zeros((1,), jnp.int32)
        return combine(masks, matching, order, whole, pairs)

    def branch(shift):
        def run(whole, parts):
            shifts = (shift, shift ^ (blocks - 1))
            pairs = [[flip(part, "chan", s) for s in shifts] for part in parts]
            order = (matching[:1, 0] != shift).astype(jnp.int32)
            return combine(masks, matching, order, whole, pairs)

        return run

    return lax.switch(pair, [branch(s) for s in range(blocks // 2)], whole, parts)


def solution(mesh):
    in_specs = (P("win", "chan", None), P(), P())
    out_specs = P(None, ("chan", "win"), None)
    return jax.shard_map(shards, mesh=mesh, in_specs=in_specs, out_specs=out_specs, check_vma=False)
```

profile of v0, /device:TPU:1, one launch (start us, length us, event | category | flops | bytes accessed | tf_op | source)
XLA Modules:
  0.0 49.2 jit_solution(13654447277705765009)
XLA Ops:
  0.0 1.0 %copy-done = bf16[1,128,1536]{2,1,0:T(8,128)(2,1)S(1)} copy-done((bf16[1,128,1536]{2,1,0:T(8,128)(2,1)S(1)}, bf16[1,128,1536]{2,1,0:T(8,128)(2,1)}, u32[]{:S(2)}) %copy-start) | copy-done | bytes 393240
  1.0 1.5 %shard_map.329 = (bf16[1,128,1536]{2,1,0:T(8,128)(2,1)S(1)}, bf16[1,128,768]{2,1,0:T(8,128)(2,1)S(1)}, bf16[1,128,768]{2,1,0:T(8,128)(2,1)S(1)}, s32[1]{0:T(128)}) custom-call(bf16[1,128,1536]{2,1,0:T(8,128)(2,1)S(1)} %copy-done, s32[4,1024]{1,0:T(4,128)} %masks_ref.1, s32[2,8]{1,0:T(2,128)} %matching_ref.1), custom_call_target="tpu_custom_call" | custom-call | tf_op jit(solution)/shard_map/pallas_call | solution.py:103
  3.1 45.1 %conditional.1 = (bf16[2,32,8192]{2,1,0:T(8,128)(2,1)S(1)}) conditional(s32[]{:T(128)} %bitcast.4, (bf16[1,128,768]{2,1,0:T(8,128)(2,1)S(1)}, bf16[1,128,768]{2,1,0:T(8,128)(2,1)S(1)}, bf16[1,128,1536]{2,1,0:T(8,128)(2,1)S(1)}, f32[64,768]{1,0:T(8,128)}, f32[64,768]{1,0:T(8,128)}, /*index=5*/s32[4,1024]{1,0:T(4,128)}, ...), branch_computations={%region_0.1_spmd, %region_1.2_spmd, %region_2.3_spmd, %region_3.4_... | conditional | flops 6442942464 | bytes 21693596 | solution.py:300
  3.4 3.1 %collective-permute-start.56 = (bf16[1,128,768]{2,1,0:T(8,128)(2,1)S(1)}, bf16[1,128,768]{2,1,0:T(8,128)(2,1)S(1)}, u32[]{:S(2)}, u32[]{:S(2)}) collective-permute-start(bf16[1,128,768]{2,1,0:T(8,128)(2,1)S(1)} %get-tuple-element.234), channel_id=1, source_target_pairs={{0,12},{4,8},{8,4},{12,0},{16,28},{20,24},{24,20},{28,16},{1,13},{... | collective-permute-start | bytes 589832 | tf_op jit(solution)/shard_map/cond/branch_3_fun/ppermute | solution.py:27
  6.5 2.3 %collective-permute-start.58 = (bf16[1,128,768]{2,1,0:T(8,128)(2,1)S(1)}, bf16[1,128,768]{2,1,0:T(8,128)(2,1)S(1)}, u32[]{:S(2)}, u32[]{:S(2)}) collective-permute-start(bf16[1,128,768]{2,1,0:T(8,128)(2,1)S(1)} %get-tuple-element.234), channel_id=1, source_target_pairs={{0,16},{4,20},{8,24},{12,28},{16,0},{20,4},{24,8},{28,12},{1,17},{... | collective-permute-start | bytes 589832 | tf_op jit(solution)/shard_map/cond/branch_3_fun/ppermute | solution.py:27
  8.9 1.3 %collective-permute-start.60 = (bf16[1,64,1536]{2,1,0:T(8,128)(2,1)S(1)}, bf16[1,64,1536]{2,1,0:T(8,128)(2,1)S(1)}, u32[]{:S(2)}, u32[]{:S(2)}) collective-permute-start(bf16[1,64,1536]{2,1,0:T(8,128)(2,1)S(1)} %get-tuple-element.303), channel_id=1, source_target_pairs={{0,2},{1,3},{2,0},{3,1},{4,6},{5,7},{6,4},{7,5},{8,10},{9,11},{10,... | collective-permute-start | bytes 589832 | tf_op jit(solution)/shard_map/cond/branch_3_fun/ppermute | solution.py:27
  10.2 3.9 %collective-permute-done.60 = bf16[1,64,1536]{2,1,0:T(8,128)(2,1)S(1)} collective-permute-done((bf16[1,64,1536]{2,1,0:T(8,128)(2,1)S(1)}, bf16[1,64,1536]{2,1,0:T(8,128)(2,1)S(1)}, u32[]{:S(2)}, u32[]{:S(2)}) %collective-permute-start.60) | collective-permute-done | bytes 196640 | tf_op jit(solution)/shard_map/cond/branch_3_fun/ppermute | solution.py:27
  14.1 2.2 %collective-permute-start.61 = (bf16[2,32,1536]{2,1,0:T(8,128)(2,1)S(1)}, bf16[2,32,1536]{2,1,0:T(8,128)(2,1)S(1)}, u32[]{:S(2)}, u32[]{:S(2)}) collective-permute-start(bf16[2,32,1536]{2,1,0:T(8,128)(2,1)S(1)} %pad_maximum_fusion.3), channel_id=1, source_target_pairs={{0,1},{1,0},{2,3},{3,2},{4,5},{5,4},{6,7},{7,6},{8,9},{9,8},{10,11... | collective-permute-start | bytes 589832 | tf_op jit(solution)/shard_map/cond/branch_3_fun/ppermute | solution.py:27
  16.4 0.1 collective-permute-start.52
  16.5 0.6 %collective-permute-start.62 = (bf16[1,128,768]{2,1,0:T(8,128)(2,1)S(1)}, bf16[1,128,768]{2,1,0:T(8,128)(2,1)S(1)}, u32[]{:S(2)}, u32[]{:S(2)}) collective-permute-start(bf16[1,128,768]{2,1,0:T(8,128)(2,1)S(1)} %collective-permute-done.56.refs_6_), channel_id=1, source_target_pairs={{0,1},{1,0},{2,3},{3,2},{4,5},{5,4},{6,7},{7,6},{8,9},{9,8},{10,11... | collective-permute-start | bytes 589832 | tf_op jit(solution)/shard_map/cond/branch_3_fun/ppermute | solution.py:27
  17.1 1.2 %collective-permute-start.57 = (bf16[1,128,768]{2,1,0:T(8,128)(2,1)S(1)}, bf16[1,128,768]{2,1,0:T(8,128)(2,1)S(1)}, u32[]{:S(2)}, u32[]{:S(2)}) collective-permute-start(bf16[1,128,768]{2,1,0:T(8,128)(2,1)S(1)} %collective-permute-done.56.refs_6_), channel_id=1, source_target_pairs={{0,2},{1,3},{2,0},{3,1},{4,6},{5,7},{6,4},{7,5},{8,10},{9,11},{10,... | collective-permute-start | bytes 589832 | tf_op jit(solution)/shard_map/cond/branch_3_fun/ppermute | solution.py:27
  18.4 2.1 %collective-permute-start.63 = (bf16[1,128,768]{2,1,0:T(8,128)(2,1)S(1)}, bf16[1,128,768]{2,1,0:T(8,128)(2,1)S(1)}, u32[]{:S(2)}, u32[]{:S(2)}) collective-permute-start(bf16[1,128,768]{2,1,0:T(8,128)(2,1)S(1)} %collective-permute-done.58.refs_8_), channel_id=1, source_target_pairs={{0,1},{1,0},{2,3},{3,2},{4,5},{5,4},{6,7},{7,6},{8,9},{9,8},{10,11... | collective-permute-start | bytes 589832 | tf_op jit(solution)/shard_map/cond/branch_3_fun/ppermute | solution.py:27
  20.5 0.3 collective-permute-start.59
  20.8 0.7 %collective-permute-done.63.refs_9_ = bf16[1,128,768]{2,1,0:T(8,128)(2,1)S(1)} collective-permute-done((bf16[1,128,768]{2,1,0:T(8,128)(2,1)S(1)}, bf16[1,128,768]{2,1,0:T(8,128)(2,1)S(1)}, u32[]{:S(2)}, u32[]{:S(2)}) %collective-permute-start.63) | collective-permute-done | bytes 196640 | tf_op jit(solution)/shard_map/cond/branch_3_fun/ppermute | solution.py:27
  21.6 3.7 %branch_3_fun.4 = (f32[2048,256]{1,0:T(8,128)S(1)}, f32[2,32,128]{2,1,0:T(8,128)S(1)}) custom-call(f32[64,768]{1,0:T(8,128)S(1)} %copy-done.13, f32[64,768]{1,0:T(8,128)S(1)} %copy-done.17, s32[4,1024]{1,0:T(4,128)S(1)} %copy-done.4, s32[2,8]{1,0:T(2,128)S(1)} %copy-done.8, bf16[1,32,1536]{2,1,0:T(8,128)(2,1)S(1)} %get-tuple-element.310.refs_4_.refs_3_, ...), custom_call_target="tpu_custom_call" | custom-call | flops 1610612736 | bytes 884736 | tf_op jit(solution)/shard_map/cond/branch_3_fun/pallas_call | solution.py:229
  25.3 1.4 %collective-permute-done.52.refs_5_ = bf16[1,128,768]{2,1,0:T(8,128)(2,1)S(1)} collective-permute-done((bf16[1,128,768]{2,1,0:T(8,128)(2,1)S(1)}, bf16[1,128,768]{2,1,0:T(8,128)(2,1)S(1)}, u32[]{:S(2)}, u32[]{:S(2)}) %collective-permute-start.52) | collective-permute-done | bytes 196640 | tf_op jit(solution)/shard_map/cond/branch_3_fun/ppermute | solution.py:27
  26.7 1.1 %collective-permute-done.54.refs_7_ = bf16[1,128,768]{2,1,0:T(8,128)(2,1)S(1)} collective-permute-done((bf16[1,128,768]{2,1,0:T(8,128)(2,1)S(1)}, bf16[1,128,768]{2,1,0:T(8,128)(2,1)S(1)}, u32[]{:S(2)}, u32[]{:S(2)}) %collective-permute-start.54) | collective-permute-done | bytes 196640 | tf_op jit(solution)/shard_map/cond/branch_3_fun/ppermute | solution.py:27
  27.8 1.2 %collective-permute-start.64 = (bf16[1,128,768]{2,1,0:T(8,128)(2,1)S(1)}, bf16[1,128,768]{2,1,0:T(8,128)(2,1)S(1)}, u32[]{:S(2)}, u32[]{:S(2)}) collective-permute-start(bf16[1,128,768]{2,1,0:T(8,128)(2,1)S(1)} %collective-permute-done.52.refs_5_), channel_id=1, source_target_pairs={{0,1},{1,0},{2,3},{3,2},{4,5},{5,4},{6,7},{7,6},{8,9},{9,8},{10,11... | collective-permute-start | bytes 589832 | tf_op jit(solution)/shard_map/cond/branch_3_fun/ppermute | solution.py:27
  29.0 1.2 %collective-permute-start.53 = (bf16[1,128,768]{2,1,0:T(8,128)(2,1)S(1)}, bf16[1,128,768]{2,1,0:T(8,128)(2,1)S(1)}, u32[]{:S(2)}, u32[]{:S(2)}) collective-permute-start(bf16[1,128,768]{2,1,0:T(8,128)(2,1)S(1)} %collective-permute-done.52.refs_5_), channel_id=1, source_target_pairs={{0,2},{1,3},{2,0},{3,1},{4,6},{5,7},{6,4},{7,5},{8,10},{9,11},{10,... | collective-permute-start | bytes 589832 | tf_op jit(solution)/shard_map/cond/branch_3_fun/ppermute | solution.py:27
  30.2 0.3 collective-permute-start.55
  30.5 2.9 %branch_3_fun.5.refs_2_ = f32[2048,256]{1,0:T(8,128)S(1)} custom-call(f32[64,768]{1,0:T(8,128)S(1)} %copy-done.13, f32[64,768]{1,0:T(8,128)S(1)} %copy-done.17, f32[2048,256]{1,0:T(8,128)S(1)} %get-tuple-element.250.refs_2_, bf16[1,32,1536]{2,1,0:T(8,128)(2,1)S(1)} %get-tuple-element.310.refs_4_.refs_3_, ...), custom_call_target="tpu_custom_call" | custom-call | flops 1610612736 | bytes 884736 | tf_op jit(solution)/shard_map/cond/branch_3_fun/pallas_call | solution.py:229
  33.4 1.1 %collective-permute-start.66 = (bf16[1,128,768]{2,1,0:T(8,128)(2,1)S(1)}, bf16[1,128,768]{2,1,0:T(8,128)(2,1)S(1)}, u32[]{:S(2)}, u32[]{:S(2)}) collective-permute-start(bf16[1,128,768]{2,1,0:T(8,128)(2,1)S(1)} %collective-permute-done.57.refs_5_), channel_id=1, source_target_pairs={{0,1},{1,0},{2,3},{3,2},{4,5},{5,4},{6,7},{7,6},{8,9},{9,8},{10,11... | collective-permute-start | bytes 589832 | tf_op jit(solution)/shard_map/cond/branch_3_fun/ppermute | solution.py:27
  34.5 0.1 collective-permute-start.67
  34.6 0.4 collective-permute-done.53.refs_7_
  34.9 4.2 %collective-permute-done.55.refs_9_ = bf16[1,128,768]{2,1,0:T(8,128)(2,1)S(1)} collective-permute-done((bf16[1,128,768]{2,1,0:T(8,128)(2,1)S(1)}, bf16[1,128,768]{2,1,0:T(8,128)(2,1)S(1)}, u32[]{:S(2)}, u32[]{:S(2)}) %collective-permute-start.55) | collective-permute-done | bytes 196640 | tf_op jit(solution)/shard_map/cond/branch_3_fun/ppermute | solution.py:27
  39.1 2.9 %branch_3_fun.6.refs_2_ = f32[2048,256]{1,0:T(8,128)S(1)} custom-call(f32[64,768]{1,0:T(8,128)S(1)} %copy-done.13, f32[64,768]{1,0:T(8,128)S(1)} %copy-done.17, f32[2048,256]{1,0:T(8,128)S(1)} %branch_3_fun.5.refs_2_, bf16[1,32,1536]{2,1,0:T(8,128)(2,1)S(1)} %get-tuple-element.307.refs_3_.refs_5_, ...), custom_call_target="tpu_custom_call" | custom-call | flops 1610612736 | bytes 884736 | tf_op jit(solution)/shard_map/cond/branch_3_fun/pallas_call | solution.py:229
  42.0 1.4 %collective-permute-start.68 = (bf16[1,128,768]{2,1,0:T(8,128)(2,1)S(1)}, bf16[1,128,768]{2,1,0:T(8,128)(2,1)S(1)}, u32[]{:S(2)}, u32[]{:S(2)}) collective-permute-start(bf16[1,128,768]{2,1,0:T(8,128)(2,1)S(1)} %collective-permute-done.53.refs_7_), channel_id=1, source_target_pairs={{0,1},{1,0},{2,3},{3,2},{4,5},{5,4},{6,7},{7,6},{8,9},{9,8},{10,11... | collective-permute-start | bytes 589832 | tf_op jit(solution)/shard_map/cond/branch_3_fun/ppermute | solution.py:27
  43.5 0.1 collective-permute-start.69
  43.6 0.5 %slice.107 = s32[1,1]{1,0:T(1,128)} slice(s32[2,8]{1,0:T(2,128)S(1)} %copy-done.8), slice={[0:1], [0:1]} | slice | bytes 8 | tf_op jit(solution)/shard_map/cond/branch_3_fun/slice | solution.py:295
  44.7 0.3 collective-permute-done.69.refs_10_
  44.9 3.1 %branch_3_fun.7 = bf16[2,32,8192]{2,1,0:T(8,128)(2,1)S(1)} custom-call(f32[64,768]{1,0:T(8,128)S(1)} %copy-done.13, f32[64,768]{1,0:T(8,128)S(1)} %copy-done.17, f32[2048,256]{1,0:T(8,128)S(1)} %branch_3_fun.6.refs_2_, f32[2,32,128]{2,1,0:T(8,128)S(1)} %get-tuple-element.267.refs_3_, s32[1]{0:T(128)} %bitcast.3.refs_4_, ...), custom_call_target="tpu_custom_call" | custom-call | flops 1610612736 | bytes 884736 | tf_op jit(solution)/shard_map/cond/branch_3_fun/pallas_call | solution.py:229
  48.3 1.0 %copy-done.9 = bf16[2,32,8192]{2,1,0:T(8,128)(2,1)} copy-done((bf16[2,32,8192]{2,1,0:T(8,128)(2,1)}, bf16[2,32,8192]{2,1,0:T(8,128)(2,1)S(1)}, u32[]{:S(2)}) %copy-start.9) | copy-done | bytes 1048600
  (28 shorter events, 0.2 us)
Async XLA Ops:
  0.0 1.0 %copy-start = (bf16[1,128,1536]{2,1,0:T(8,128)(2,1)S(1)}, bf16[1,128,1536]{2,1,0:T(8,128)(2,1)}, u32[]{:S(2)}) copy-start(bf16[1,128,1536]{2,1,0:T(8,128)(2,1)} %spectra_ref.1) | copy-start | bytes 1179652
  3.3 18.2 %copy-start.4 = (s32[4,1024]{1,0:T(4,128)S(1)}, s32[4,1024]{1,0:T(4,128)}, u32[]{:S(2)}) copy-start(s32[4,1024]{1,0:T(4,128)} %get-tuple-element.237.refs_2_) | copy-start | bytes 49156 | tf_op jit(solution)/shard_map/cond
  3.3 18.2 %copy-start.8 = (s32[2,8]{1,0:T(2,128)S(1)}, s32[2,8]{1,0:T(2,128)}, u32[]{:S(2)}) copy-start(s32[2,8]{1,0:T(2,128)} %get-tuple-element.238.refs_3_) | copy-start | bytes 196 | tf_op jit(solution)/shard_map/cond
  3.4 18.2 %copy-start.13 = (f32[64,768]{1,0:T(8,128)S(1)}, f32[64,768]{1,0:T(8,128)}, u32[]{:S(2)}) copy-start(f32[64,768]{1,0:T(8,128)} %get-tuple-element.231.refs_0_) | copy-start | bytes 589828 | tf_op jit(solution)/shard_map/cond
  3.4 18.2 %copy-start.17 = (f32[64,768]{1,0:T(8,128)S(1)}, f32[64,768]{1,0:T(8,128)}, u32[]{:S(2)}) copy-start(f32[64,768]{1,0:T(8,128)} %get-tuple-element.232.refs_1_) | copy-start | bytes 589828 | tf_op jit(solution)/shard_map/cond
  3.4 13.1 %collective-permute-start.56 = (bf16[1,128,768]{2,1,0:T(8,128)(2,1)S(1)}, bf16[1,128,768]{2,1,0:T(8,128)(2,1)S(1)}, u32[]{:S(2)}, u32[]{:S(2)}) collective-permute-start(bf16[1,128,768]{2,1,0:T(8,128)(2,1)S(1)} %get-tuple-element.234), channel_id=1, source_target_pairs={{0,12},{4,8},{8,4},{12,0},{16,28},{20,24},{24,20},{28,16},{1,13},{... | collective-permute-start | bytes 589832 | tf_op jit(solution)/shard_map/cond/branch_3_fun/ppermute | solution.py:27
  6.5 10.6 %collective-permute-start.58 = (bf16[1,128,768]{2,1,0:T(8,128)(2,1)S(1)}, bf16[1,128,768]{2,1,0:T(8,128)(2,1)S(1)}, u32[]{:S(2)}, u32[]{:S(2)}) collective-permute-start(bf16[1,128,768]{2,1,0:T(8,128)(2,1)S(1)} %get-tuple-element.234), channel_id=1, source_target_pairs={{0,16},{4,20},{8,24},{12,28},{16,0},{20,4},{24,8},{28,12},{1,17},{... | collective-permute-start | bytes 589832 | tf_op jit(solution)/shard_map/cond/branch_3_fun/ppermute | solution.py:27
  8.9 5.2 %collective-permute-start.60 = (bf16[1,64,1536]{2,1,0:T(8,128)(2,1)S(1)}, bf16[1,64,1536]{2,1,0:T(8,128)(2,1)S(1)}, u32[]{:S(2)}, u32[]{:S(2)}) collective-permute-start(bf16[1,64,1536]{2,1,0:T(8,128)(2,1)S(1)} %get-tuple-element.303), channel_id=1, source_target_pairs={{0,2},{1,3},{2,0},{3,1},{4,6},{5,7},{6,4},{7,5},{8,10},{9,11},{10,... | collective-permute-start | bytes 589832 | tf_op jit(solution)/shard_map/cond/branch_3_fun/ppermute | solution.py:27
  14.1 4.3 %collective-permute-start.61 = (bf16[2,32,1536]{2,1,0:T(8,128)(2,1)S(1)}, bf16[2,32,1536]{2,1,0:T(8,128)(2,1)S(1)}, u32[]{:S(2)}, u32[]{:S(2)}) collective-permute-start(bf16[2,32,1536]{2,1,0:T(8,128)(2,1)S(1)} %pad_maximum_fusion.3), channel_id=1, source_target_pairs={{0,1},{1,0},{2,3},{3,2},{4,5},{5,4},{6,7},{7,6},{8,9},{9,8},{10,11... | collective-permute-start | bytes 589832 | tf_op jit(solution)/shard_map/cond/branch_3_fun/ppermute | solution.py:27
  16.4 10.4 %collective-permute-start.52 = (bf16[1,128,768]{2,1,0:T(8,128)(2,1)S(1)}, bf16[1,128,768]{2,1,0:T(8,128)(2,1)S(1)}, u32[]{:S(2)}, u32[]{:S(2)}) collective-permute-start(bf16[1,128,768]{2,1,0:T(8,128)(2,1)S(1)} %get-tuple-element.233), channel_id=1, source_target_pairs={{0,12},{4,8},{8,4},{12,0},{16,28},{20,24},{24,20},{28,16},{1,13},{... | collective-permute-start | bytes 589832 | tf_op jit(solution)/shard_map/cond/branch_3_fun/ppermute | solution.py:27
  16.5 11.3 %collective-permute-start.54 = (bf16[1,128,768]{2,1,0:T(8,128)(2,1)S(1)}, bf16[1,128,768]{2,1,0:T(8,128)(2,1)S(1)}, u32[]{:S(2)}, u32[]{:S(2)}) collective-permute-start(bf16[1,128,768]{2,1,0:T(8,128)(2,1)S(1)} %get-tuple-element.233), channel_id=1, source_target_pairs={{0,16},{4,20},{8,24},{12,28},{16,0},{20,4},{24,8},{28,12},{1,17},{... | collective-permute-start | bytes 589832 | tf_op jit(solution)/shard_map/cond/branch_3_fun/ppermute | solution.py:27
  16.5 4.0 %collective-permute-start.62 = (bf16[1,128,768]{2,1,0:T(8,128)(2,1)S(1)}, bf16[1,128,768]{2,1,0:T(8,128)(2,1)S(1)}, u32[]{:S(2)}, u32[]{:S(2)}) collective-permute-start(bf16[1,128,768]{2,1,0:T(8,128)(2,1)S(1)} %collective-permute-done.56.refs_6_), channel_id=1, source_target_pairs={{0,1},{1,0},{2,3},{3,2},{4,5},{5,4},{6,7},{7,6},{8,9},{9,8},{10,11... | collective-permute-start | bytes 589832 | tf_op jit(solution)/shard_map/cond/branch_3_fun/ppermute | solution.py:27
  17.1 13.0 %collective-permute-start.57 = (bf16[1,128,768]{2,1,0:T(8,128)(2,1)S(1)}, bf16[1,128,768]{2,1,0:T(8,128)(2,1)S(1)}, u32[]{:S(2)}, u32[]{:S(2)}) collective-permute-start(bf16[1,128,768]{2,1,0:T(8,128)(2,1)S(1)} %collective-permute-done.56.refs_6_), channel_id=1, source_target_pairs={{0,2},{1,3},{2,0},{3,1},{4,6},{5,7},{6,4},{7,5},{8,10},{9,11},{10,... | collective-permute-start | bytes 589832 | tf_op jit(solution)/shard_map/cond/branch_3_fun/ppermute | solution.py:27
  18.4 3.2 %collective-permute-start.63 = (bf16[1,128,768]{2,1,0:T(8,128)(2,1)S(1)}, bf16[1,128,768]{2,1,0:T(8,128)(2,1)S(1)}, u32[]{:S(2)}, u32[]{:S(2)}) collective-permute-start(bf16[1,128,768]{2,1,0:T(8,128)(2,1)S(1)} %collective-permute-done.58.refs_8_), channel_id=1, source_target_pairs={{0,1},{1,0},{2,3},{3,2},{4,5},{5,4},{6,7},{7,6},{8,9},{9,8},{10,11... | collective-permute-start | bytes 589832 | tf_op jit(solution)/shard_map/cond/branch_3_fun/ppermute | solution.py:27
  20.5 9.9 %collective-permute-start.59 = (bf16[1,128,768]{2,1,0:T(8,128)(2,1)S(1)}, bf16[1,128,768]{2,1,0:T(8,128)(2,1)S(1)}, u32[]{:S(2)}, u32[]{:S(2)}) collective-permute-start(bf16[1,128,768]{2,1,0:T(8,128)(2,1)S(1)} %collective-permute-done.58.refs_8_), channel_id=1, source_target_pairs={{0,2},{1,3},{2,0},{3,1},{4,6},{5,7},{6,4},{7,5},{8,10},{9,11},{10,... | collective-permute-start | bytes 589832 | tf_op jit(solution)/shard_map/cond/branch_3_fun/ppermute | solution.py:27
  27.8 2.7 %collective-permute-start.64 = (bf16[1,128,768]{2,1,0:T(8,128)(2,1)S(1)}, bf16[1,128,768]{2,1,0:T(8,128)(2,1)S(1)}, u32[]{:S(2)}, u32[]{:S(2)}) collective-permute-start(bf16[1,128,768]{2,1,0:T(8,128)(2,1)S(1)} %collective-permute-done.52.refs_5_), channel_id=1, source_target_pairs={{0,1},{1,0},{2,3},{3,2},{4,5},{5,4},{6,7},{7,6},{8,9},{9,8},{10,11... | collective-permute-start | bytes 589832 | tf_op jit(solution)/shard_map/cond/branch_3_fun/ppermute | solution.py:27
  29.0 1.5 %collective-permute-start.65 = (bf16[1,128,768]{2,1,0:T(8,128)(2,1)S(1)}, bf16[1,128,768]{2,1,0:T(8,128)(2,1)S(1)}, u32[]{:S(2)}, u32[]{:S(2)}) collective-permute-start(bf16[1,128,768]{2,1,0:T(8,128)(2,1)S(1)} %collective-permute-done.54.refs_7_), channel_id=1, source_target_pairs={{0,1},{1,0},{2,3},{3,2},{4,5},{5,4},{6,7},{7,6},{8,9},{9,8},{10,11... | collective-permute-start | bytes 589832 | tf_op jit(solution)/shard_map/cond/branch_3_fun/ppermute | solution.py:27
  29.0 6.0 %collective-permute-start.53 = (bf16[1,128,768]{2,1,0:T(8,128)(2,1)S(1)}, bf16[1,128,768]{2,1,0:T(8,128)(2,1)S(1)}, u32[]{:S(2)}, u32[]{:S(2)}) collective-permute-start(bf16[1,128,768]{2,1,0:T(8,128)(2,1)S(1)} %collective-permute-done.52.refs_5_), channel_id=1, source_target_pairs={{0,2},{1,3},{2,0},{3,1},{4,6},{5,7},{6,4},{7,5},{8,10},{9,11},{10,... | collective-permute-start | bytes 589832 | tf_op jit(solution)/shard_map/cond/branch_3_fun/ppermute | solution.py:27
  30.2 9.0 %collective-permute-start.55 = (bf16[1,128,768]{2,1,0:T(8,128)(2,1)S(1)}, bf16[1,128,768]{2,1,0:T(8,128)(2,1)S(1)}, u32[]{:S(2)}, u32[]{:S(2)}) collective-permute-start(bf16[1,128,768]{2,1,0:T(8,128)(2,1)S(1)} %collective-permute-done.54.refs_7_), channel_id=1, source_target_pairs={{0,2},{1,3},{2,0},{3,1},{4,6},{5,7},{6,4},{7,5},{8,10},{9,11},{10,... | collective-permute-start | bytes 589832 | tf_op jit(solution)/shard_map/cond/branch_3_fun/ppermute | solution.py:27
  33.4 5.8 %collective-permute-start.66 = (bf16[1,128,768]{2,1,0:T(8,128)(2,1)S(1)}, bf16[1,128,768]{2,1,0:T(8,128)(2,1)S(1)}, u32[]{:S(2)}, u32[]{:S(2)}) collective-permute-start(bf16[1,128,768]{2,1,0:T(8,128)(2,1)S(1)} %collective-permute-done.57.refs_5_), channel_id=1, source_target_pairs={{0,1},{1,0},{2,3},{3,2},{4,5},{5,4},{6,7},{7,6},{8,9},{9,8},{10,11... | collective-permute-start | bytes 589832 | tf_op jit(solution)/shard_map/cond/branch_3_fun/ppermute | solution.py:27
  34.5 4.7 %collective-permute-start.67 = (bf16[1,128,768]{2,1,0:T(8,128)(2,1)S(1)}, bf16[1,128,768]{2,1,0:T(8,128)(2,1)S(1)}, u32[]{:S(2)}, u32[]{:S(2)}) collective-permute-start(bf16[1,128,768]{2,1,0:T(8,128)(2,1)S(1)} %collective-permute-done.59.refs_7_), channel_id=1, source_target_pairs={{0,1},{1,0},{2,3},{3,2},{4,5},{5,4},{6,7},{7,6},{8,9},{9,8},{10,11... | collective-permute-start | bytes 589832 | tf_op jit(solution)/shard_map/cond/branch_3_fun/ppermute | solution.py:27
  42.0 2.6 %collective-permute-start.68 = (bf16[1,128,768]{2,1,0:T(8,128)(2,1)S(1)}, bf16[1,128,768]{2,1,0:T(8,128)(2,1)S(1)}, u32[]{:S(2)}, u32[]{:S(2)}) collective-permute-start(bf16[1,128,768]{2,1,0:T(8,128)(2,1)S(1)} %collective-permute-done.53.refs_7_), channel_id=1, source_target_pairs={{0,1},{1,0},{2,3},{3,2},{4,5},{5,4},{6,7},{7,6},{8,9},{9,8},{10,11... | collective-permute-start | bytes 589832 | tf_op jit(solution)/shard_map/cond/branch_3_fun/ppermute | solution.py:27
  43.5 1.4 %collective-permute-start.69 = (bf16[1,128,768]{2,1,0:T(8,128)(2,1)S(1)}, bf16[1,128,768]{2,1,0:T(8,128)(2,1)S(1)}, u32[]{:S(2)}, u32[]{:S(2)}) collective-permute-start(bf16[1,128,768]{2,1,0:T(8,128)(2,1)S(1)} %collective-permute-done.55.refs_9_), channel_id=1, source_target_pairs={{0,1},{1,0},{2,3},{3,2},{4,5},{5,4},{6,7},{7,6},{8,9},{9,8},{10,11... | collective-permute-start | bytes 589832 | tf_op jit(solution)/shard_map/cond/branch_3_fun/ppermute | solution.py:27
  48.2 1.0 %copy-start.9 = (bf16[2,32,8192]{2,1,0:T(8,128)(2,1)}, bf16[2,32,8192]{2,1,0:T(8,128)(2,1)S(1)}, u32[]{:S(2)}) copy-start(bf16[2,32,8192]{2,1,0:T(8,128)(2,1)S(1)} %get-tuple-element.455) | copy-start | bytes 3145732
where the time goes:
time: 49.7 us; the launch traced here: 49.2 us
  starting transfers between devices  18.8 us (38%)
  Pallas kernels  14 us (28%)
  waiting for transfers between devices  12 us (24%)
  local copies, waits for them, and re-layouts  2.51 us (5%)
  loops' own time  1.13 us (2%)
  between operations  0.68 us (1%)
    ppermute x18, starting transfers between devices, flip(): lax.ppermute(value, axis, [(i, i ^ bits) for i in range(lax.axis_size(axi...  18.8 us
    pallas_call x4, Pallas kernels, correlate(): pl.pallas_call(functools.partial(correlate_kernel, plan, first, last), ou...  12.6 us
    ppermute x18, waiting for transfers between devices, flip(): lax.ppermute(value, axis, [(i, i ^ bits) for i in range(lax.axis_size(axi...  12 us
    unnamed x4, local copies, waits for them, and re-layouts  1.96 us
    pallas_call x1, Pallas kernels, prepare(): pl.pallas_call(prepare_kernel, out_shape=[shape(spectra.shape, jnp.bfloat...  1.46 us
    another operation x1, loops' own time, shards(): lax.switch(pair, [branch(s) for s in range(blocks // 2)], whole, parts)  1.13 us
  transfers between devices with their start and end apart: 18, of which 7 were waited for; matrix products, arithmetic and copies ran while one was open for 1% of the time, Pallas kernels for 13%

commit v1 on v0

--- a/solution.py
+++ b/solution.py
@@ -37,7 +37,11 @@
     return [1 << k for k in reversed(range(size.bit_length() - 1))]
 
 
-def own_rows(values):
+def after(values, state):
+    return lax.optimization_barrier((values, state))
+
+
+def own_rows(values, later):
     held = {0: values}
     count = values.shape[0]
     for bit in descending_bits(lax.axis_size("win")):
@@ -50,18 +54,12 @@
             sent[d] = jnp.where(upper, low, high)
         keys = list(held)
         moved = flip(jnp.concatenate([sent[d] for d in keys], axis=0), "win", bit)
+        if len(keys) == 1 and later is not None:
+            moved, later = after(moved, later)
         for n, d in enumerate(keys):
             kept[d | bit] = moved[n * count : (n + 1) * count]
         held = kept
-    return held
-
-
-def gather_windows(values):
-    held = {0: values}
-    for bit in descending_bits(lax.axis_size("win")):
-        for d in list(held):
-            held[d | bit] = flip(held[d], "win", bit)
-    return held
+    return held, later
 
 
 def prepare_kernel(spectra_ref, masks_ref, matching_ref, whole_ref, *refs):
@@ -110,7 +108,7 @@
     return outs[0], outs[1:-1], outs[-1][0]
 
 
-def correlate_kernel(plan, first, last, *refs):
+def correlate_kernel(plan, shift, first, last, *refs):
     refs = list(refs)
     take = lambda count: [refs.pop(0) for _ in range(count)]
     cos_ref, sin_ref = take(2)
@@ -119,11 +117,11 @@
     else:
         (total_ref,) = take(1)
     if last:
-        scale_ref, order_ref = take(2)
+        scale_ref, matching_ref = take(2)
     own_refs = take(1 + max(piece[0] for piece in plan))
-    left_refs = take(len(plan))
-    right_refs = take(len(plan))
-    rows, block = own_refs[0].shape[1], left_refs[0].shape[1]
+    stack_refs = take(len(plan))
+    w_count, rows, _ = own_refs[0].shape
+    block = stack_refs[0].shape[1]
     bins = own_refs[0].shape[2] // 2
 
     def dot(lhs, rhs):
@@ -149,7 +147,8 @@
             new_scale_ref[r] = counts_ref[pl.ds(pl.multiple_of(slot * rows, rows), rows), :]
     out_ref = refs[0]
     if last:
-        swapped = order_ref[0]
+        stage_ref, copy_sems = refs[1], refs[2]
+        swapped = 0 if shift is None else jnp.where(matching_ref[0, 0] == shift, 0, 1)
         rounds = [swapped, 1 - swapped]
         scales = [scale_ref[r] for r in rounds]
 
@@ -157,7 +156,7 @@
         step = pl.multiple_of(index * LAG_STEP, LAG_STEP)
         total = None
         for n, (own_at, first_bin, width) in enumerate(plan):
-            for q in range(own_refs[0].shape[0]):
+            for q in range(w_count):
                 for c in range(0, width, BIN_STEP):
                     size = min(BIN_STEP, width - c)
                     b = first_bin + c
@@ -173,7 +172,10 @@
                     for side in range(2):
                         at = side * width + c
                         rhs = jnp.concatenate(
-                            [ref[q, :, at : at + size] for ref in (left_refs[n], right_refs[n])],
+                            [
+                                stack_refs[n][r * w_count + q, :, at : at + size]
+                                for r in range(ROUNDS)
+                            ],
                             axis=0,
                         )
                         term = dot(jnp.concatenate(turned[side], axis=0), rhs)
@@ -188,22 +190,33 @@
             lanes = pl.ds(pl.multiple_of((step + t) * block, block), block)
             for side in range(ROUNDS):
                 part = total[t * rows : (t + 1) * rows, side * block : (side + 1) * block]
-                out_ref[rounds[side], :, lanes] = (part * scales[side]).astype(jnp.bfloat16)
+                stage_ref[rounds[side], :, lanes] = (part * scales[side]).astype(jnp.bfloat16)
+        copy(index).start()
         return carry
 
+    def copy(index):
+        size = LAG_STEP * block
+        lanes = pl.ds(pl.multiple_of(index * size, size), size)
+        return pltpu.make_async_copy(
+            stage_ref.at[:, :, lanes], out_ref.at[:, :, lanes], copy_sems.at[index]
+        )
+
     lax.fori_loop(0, LAGS // LAG_STEP, one_step, 0)
-
-
-def correlate(state, masks, matching, order, pieces, last):
+    if last:
+        for index in range(LAGS // LAG_STEP):
+            copy(index).wait()
+
+
+def correlate(state, masks, matching, shift, pieces, last):
     first = state is None
     own, plan = [], []
-    for rows, first_bin, pair in pieces:
+    for rows, first_bin, stack in pieces:
         if not any(rows is seen for seen in own):
             own.append(rows)
         at = next(n for n, seen in enumerate(own) if seen is rows)
-        plan.append((at, first_bin, pair[0].shape[2] // 2))
-    _, rows, two_bins = own[0].shape
-    block = pieces[0][2][0].shape[1]
+        plan.append((at, first_bin, stack.shape[2] // 2))
+    w_count, rows, two_bins = own[0].shape
+    block = pieces[0][2].shape[1]
     cos, sin = tables(two_bins // 2)
     arrays = [jnp.asarray(cos), jnp.asarray(sin)]
     specs = [VMEM] * 2
@@ -214,24 +227,31 @@
         arrays.append(state[0])
         specs.append(VMEM)
     if last:
-        arrays += [state[1], order]
+        arrays += [state[1], matching]
         specs += [VMEM, SMEM]
-    others = own + [pair[0] for *_, pair in pieces] + [pair[1] for *_, pair in pieces]
+    others = own + [stack for *_, stack in pieces]
     shape = jax.ShapeDtypeStruct
     running = shape((LAGS * rows, ROUNDS * block), jnp.float32)
-    if last:
-        outs = [shape((ROUNDS, rows, LAGS * block), jnp.bfloat16)]
+    scratch = []
+    if last:
+        final = shape((ROUNDS, rows, LAGS * block), jnp.bfloat16)
+        outs, out_specs = [final], [pl.BlockSpec(memory_space=pl.ANY)]
+        scratch = [
+            pltpu.VMEM(final.shape, final.dtype),
+            pltpu.SemaphoreType.DMA((LAGS // LAG_STEP,)),
+        ]
     elif first:
-        outs = [running, shape((ROUNDS, rows, block), jnp.float32)]
+        outs, out_specs = [running, shape((ROUNDS, rows, block), jnp.float32)], [VMEM] * 2
+        scratch = [pltpu.VMEM((block, block), jnp.float32)]
     else:
-        outs = [running]
-    depth = 2 * sum(own[0].shape[0] * width for _, _, width in plan)
+        outs, out_specs = [running], [VMEM]
+    depth = 2 * sum(w_count * width for _, _, width in plan)
     result = pl.pallas_call(
-        functools.partial(correlate_kernel, plan, first, last),
+        functools.partial(correlate_kernel, plan, shift, first, last),
         out_shape=outs,
         in_specs=specs + [VMEM] * len(others),
-        out_specs=[VMEM] * len(outs),
-        scratch_shapes=[pltpu.VMEM((block, block), jnp.float32)] if first else [],
+        out_specs=out_specs,
+        scratch_shapes=scratch,
         compiler_params=PARAMS,
         cost_estimate=pl.CostEstimate(
             flops=2 * LAGS * rows * depth * ROUNDS * block,
@@ -244,33 +264,34 @@
     return (result[0], result[1] if first else state[1])
 
 
-def after(values, state):
-    return lax.optimization_barrier((values, state))
-
-
-def combine(masks, matching, order, whole, pairs):
-    own = own_rows(whole)
-    width = pairs[0][0].shape[2] // 2
-    low = [bit for bit in descending_bits(lax.axis_size("win"))][-1]
-    high = descending_bits(lax.axis_size("win"))[:-1]
-    state = None
-    held = {0: pairs}
-    for bit in high:
-        held |= {
-            d | bit: [[flip(side, "win", bit) for side in pair] for pair in held[d]] for d in list(held)
-        }
-    steps = [(d, n) for d in sorted(held) for n in range(len(pairs))]
+def combine(masks, matching, shift, own, sides):
+    width = sides[0][0].shape[2] // 2
+    low = descending_bits(lax.axis_size("win"))[-1]
+    steps = [(d, n) for d in sorted(own) if not d & low for n in range(len(sides))]
+    state, held = None, {}
+
+    def stack(d, n, state):
+        if (d, n) not in held:
+            if d == 0:
+                pair = sides[n]
+                if state is not None:
+                    pair, state = after(pair, state)
+                held[d, n] = jnp.concatenate(pair, axis=0)
+            else:
+                bit = d & -d
+                before, state = stack(d ^ bit, n, state)
+                held[d, n] = flip(before, "win", bit)
+        return held[d, n], state
+
     for number, (d, n) in enumerate(steps):
-        pair = held[d][n]
-        if state is not None:
-            pair, state = after(pair, state)
-        across = [flip(side, "win", low) for side in pair]
+        here, state = stack(d, n, state)
+        across = flip(here, "win", low)
         ahead = number + 1
         if 0 < number and ahead < len(steps) and steps[ahead][0] != 0:
-            d_ahead, n_ahead = steps[ahead]
-            (held[d_ahead][n_ahead], across), state = after((held[d_ahead][n_ahead], across), state)
-        pieces = [(own[d], n * width, pair), (own[d | low], n * width, across)]
-        state = correlate(state, masks, matching, order, pieces, ahead == len(steps))
+            coming, state = stack(*steps[ahead], state)
+            (held[steps[ahead]], across), state = after((coming, across), state)
+        pieces = [(own[d], n * width, here), (own[d | low], n * width, across)]
+        state = correlate(state, masks, matching, shift, pieces, ahead == len(steps))
     return state
 
 
@@ -279,21 +300,22 @@
     whole, parts, pair = prepare(spectra, masks, matching)
 
     if blocks > SWITCH_BLOCKS:
-        pairs = [[part, part] for part in parts]
-        for bit in range(blocks.bit_length() - 1):
-            taken = (matching[0, 0] >> bit) & 1 == 1
-            for n, (left, right) in enumerate(pairs):
+        sides = []
+        for part in parts:
+            left = right = part
+            for bit in range(blocks.bit_length() - 1):
+                taken = (matching[0, 0] >> bit) & 1 == 1
                 moved = flip(jnp.where(taken, left, right), "chan", 1 << bit)
-                pairs[n] = [jnp.where(taken, moved, left), jnp.where(taken, right, moved)]
-        order = jnp.zeros((1,), jnp.int32)
-        return combine(masks, matching, order, whole, pairs)
+                left, right = jnp.where(taken, moved, left), jnp.where(taken, right, moved)
+            sides.append([left, right])
+        return combine(masks, matching, None, own_rows(whole, None)[0], sides)
 
     def branch(shift):
         def run(whole, parts):
+            own, later = own_rows(whole, parts[1:])
             shifts = (shift, shift ^ (blocks - 1))
-            pairs = [[flip(part, "chan", s) for s in shifts] for part in parts]
-            order = (matching[:1, 0] != shift).astype(jnp.int32)
-            return combine(masks, matching, order, whole, pairs)
+            sides = [[flip(part, "chan", s) for s in shifts] for part in (parts[0], *later)]
+            return combine(masks, matching, shift, own, sides)
 
         return run
 

time: 49.7 us -> 47 us (0.946)
  the two profiles are of different devices: /device:TPU:1 before, /device:TPU:17 now
where the time goes in v1:
time: 47 us; the launch traced here: 46.8 us
  starting transfers between devices  16.5 us (35%)
  Pallas kernels  14.7 us (31%)
  waiting for transfers between devices  12.3 us (26%)
  local copies, waits for them, and re-layouts  2.06 us (4%)
  between operations  0.68 us (1%)
    ppermute x12, starting transfers between devices, flip(): lax.ppermute(value, axis, [(i, i ^ bits) for i in range(lax.axis_size(axi...  16.5 us
    pallas_call x4, Pallas kernels, correlate(): pl.pallas_call(functools.partial(correlate_kernel, plan, shift, first, la...  13.3 us
    ppermute x12, waiting for transfers between devices, flip(): lax.ppermute(value, axis, [(i, i ^ bits) for i in range(lax.axis_size(axi...  12.3 us
    unnamed x4, local copies, waits for them, and re-layouts  1.96 us
    pallas_call x1, Pallas kernels, prepare(): pl.pallas_call(prepare_kernel, out_shape=[shape(spectra.shape, jnp.bfloat...  1.46 us
  transfers between devices with their start and end apart: 12, of which 4 were waited for; matrix products, arithmetic and copies ran while one was open for 0% of the time, Pallas kernels for 20%

profile of v1, /device:TPU:17, one launch (start us, length us, event | category | flops | bytes accessed | tf_op | source)
XLA Modules:
  0.0 46.8 jit_solution(10255292461232071165)
XLA Ops:
  0.0 1.0 %copy-done = bf16[1,128,1536]{2,1,0:T(8,128)(2,1)S(1)} copy-done((bf16[1,128,1536]{2,1,0:T(8,128)(2,1)S(1)}, bf16[1,128,1536]{2,1,0:T(8,128)(2,1)}, u32[]{:S(2)}) %copy-start) | copy-done | bytes 393240
  1.0 1.5 %shard_map.329 = (bf16[1,128,1536]{2,1,0:T(8,128)(2,1)S(1)}, bf16[1,128,768]{2,1,0:T(8,128)(2,1)S(1)}, bf16[1,128,768]{2,1,0:T(8,128)(2,1)S(1)}, s32[1]{0:T(128)}) custom-call(bf16[1,128,1536]{2,1,0:T(8,128)(2,1)S(1)} %copy-done, s32[4,1024]{1,0:T(4,128)} %masks_ref.1, s32[2,8]{1,0:T(2,128)} %matching_ref.1), custom_call_target="tpu_custom_call" | custom-call | tf_op jit(solution)/shard_map/pallas_call | solution.py:101
  3.1 42.7 %conditional.1 = (bf16[2,32,8192]{2,1,0:T(8,128)(2,1)S(1)}) conditional(s32[]{:T(128)} %bitcast, (bf16[1,128,1536]{2,1,0:T(8,128)(2,1)S(1)}, bf16[1,128,768]{2,1,0:T(8,128)(2,1)S(1)}, bf16[1,128,768]{2,1,0:T(8,128)(2,1)S(1)}, f32[64,768]{1,0:T(8,128)}, f32[64,768]{1,0:T(8,128)}, /*index=5*/s32[4,1024]{1,0:T(4,128)}, ...), branch_computations={%region_0.1_spmd, %region_1.2_spmd, %region_2.3_spmd, %region_3.4_... | conditional | flops 6442942464 | bytes 23266200 | solution.py:322
  3.1 0.0 copy-start.2
  3.2 0.0 copy-start.6
  3.2 0.0 copy-start.11
  3.2 0.0 copy-start.15
  3.2 0.2 collective-permute-start.15
  3.4 1.2 %collective-permute-start.14 = (bf16[1,128,768]{2,1,0:T(8,128)(2,1)S(1)}, bf16[1,128,768]{2,1,0:T(8,128)(2,1)S(1)}, u32[]{:S(2)}, u32[]{:S(2)}) collective-permute-start(bf16[1,128,768]{2,1,0:T(8,128)(2,1)S(1)} %get-tuple-element.155), channel_id=1, source_target_pairs={{0,4},{4,0},{8,12},{12,8},{16,20},{20,16},{24,28},{28,24},{1,5},{5... | collective-permute-start | bytes 589832 | tf_op jit(solution)/shard_map/cond/branch_1_fun/ppermute | solution.py:27
  4.7 1.3 %collective-permute-start.10 = (bf16[1,64,1536]{2,1,0:T(8,128)(2,1)S(1)}, bf16[1,64,1536]{2,1,0:T(8,128)(2,1)S(1)}, u32[]{:S(2)}, u32[]{:S(2)}) collective-permute-start(bf16[1,64,1536]{2,1,0:T(8,128)(2,1)S(1)} %get-tuple-element.248), channel_id=1, source_target_pairs={{0,2},{1,3},{2,0},{3,1},{4,6},{5,7},{6,4},{7,5},{8,10},{9,11},{10,... | collective-permute-start | bytes 589832 | tf_op jit(solution)/shard_map/cond/branch_1_fun/ppermute | solution.py:27
  6.0 3.9 %collective-permute-done.10 = bf16[1,64,1536]{2,1,0:T(8,128)(2,1)S(1)} collective-permute-done((bf16[1,64,1536]{2,1,0:T(8,128)(2,1)S(1)}, bf16[1,64,1536]{2,1,0:T(8,128)(2,1)S(1)}, u32[]{:S(2)}, u32[]{:S(2)}) %collective-permute-start.10) | collective-permute-done | bytes 196640 | tf_op jit(solution)/shard_map/cond/branch_1_fun/ppermute | solution.py:27
  9.9 1.3 %collective-permute-start.12 = (bf16[1,128,768]{2,1,0:T(8,128)(2,1)S(1)}, bf16[1,128,768]{2,1,0:T(8,128)(2,1)S(1)}, u32[]{:S(2)}, u32[]{:S(2)}) collective-permute-start(bf16[1,128,768]{2,1,0:T(8,128)(2,1)S(1)} %get-tuple-element.149), channel_id=1, source_target_pairs={{0,24},{4,28},{8,16},{12,20},{16,8},{20,12},{24,0},{28,4},{1,25},{... | collective-permute-start | bytes 589832 | tf_op jit(solution)/shard_map/cond/branch_1_fun/ppermute | solution.py:27
  11.2 0.2 collective-permute-start.11
  11.5 2.8 %collective-permute-start.13 = (bf16[2,32,1536]{2,1,0:T(8,128)(2,1)S(1)}, bf16[2,32,1536]{2,1,0:T(8,128)(2,1)S(1)}, u32[]{:S(2)}, u32[]{:S(2)}) collective-permute-start(bf16[2,32,1536]{2,1,0:T(8,128)(2,1)S(1)} %pad_maximum_fusion.1), channel_id=1, source_target_pairs={{0,1},{1,0},{2,3},{3,2},{4,5},{5,4},{6,7},{7,6},{8,9},{9,8},{10,11... | collective-permute-start | bytes 589832 | tf_op jit(solution)/shard_map/cond/branch_1_fun/ppermute | solution.py:27
  14.3 0.0 collective-permute-done.15
  14.3 1.3 %collective-permute-start.18 = (bf16[2,128,768]{2,1,0:T(8,128)(2,1)S(1)}, bf16[2,128,768]{2,1,0:T(8,128)(2,1)S(1)}, u32[]{:S(2)}, u32[]{:S(2)}) collective-permute-start(bf16[2,128,768]{2,1,0:T(8,128)(2,1)S(1)} %constant_dynamic-update-slice_fusion.4.refs_6_), channel_id=1, source_target_pairs={{0,2},{1,3},{2,0},{3,1},{4,6},{5,7},{6,4},{7,5},{8,10},{9,11},{10,... | collective-permute-start | bytes 1179656 | tf_op jit(solution)/shard_map/cond/branch_1_fun/ppermute | solution.py:27
  15.6 6.1 %collective-permute-start.16 = (bf16[2,128,768]{2,1,0:T(8,128)(2,1)S(1)}, bf16[2,128,768]{2,1,0:T(8,128)(2,1)S(1)}, u32[]{:S(2)}, u32[]{:S(2)}) collective-permute-start(bf16[2,128,768]{2,1,0:T(8,128)(2,1)S(1)} %constant_dynamic-update-slice_fusion.4.refs_6_), channel_id=1, source_target_pairs={{0,1},{1,0},{2,3},{3,2},{4,5},{5,4},{6,7},{7,6},{8,9},{9,8},{10,11... | collective-permute-start | bytes 1179656 | tf_op jit(solution)/shard_map/cond/branch_1_fun/ppermute | solution.py:27
  21.7 0.0 collective-permute-done.13
  21.7 1.3 %collective-permute-done.16.refs_7_ = bf16[2,128,768]{2,1,0:T(8,128)(2,1)S(1)} collective-permute-done((bf16[2,128,768]{2,1,0:T(8,128)(2,1)S(1)}, bf16[2,128,768]{2,1,0:T(8,128)(2,1)S(1)}, u32[]{:S(2)}, u32[]{:S(2)}) %collective-permute-start.16) | collective-permute-done | bytes 393248 | tf_op jit(solution)/shard_map/cond/branch_1_fun/ppermute | solution.py:27
  23.1 3.7 %branch_1_fun.4 = (f32[2048,256]{1,0:T(8,128)S(1)}, f32[2,32,128]{2,1,0:T(8,128)S(1)}) custom-call(f32[64,768]{1,0:T(8,128)S(1)} %copy-done.15, f32[64,768]{1,0:T(8,128)S(1)} %copy-done.11, s32[4,1024]{1,0:T(4,128)S(1)} %copy-done.2, s32[2,8]{1,0:T(2,128)S(1)} %copy-done.6, bf16[1,32,1536]{2,1,0:T(8,128)(2,1)S(1)} %get-tuple-element.254.refs_4_.refs_3_, ...), custom_call_target="tpu_custom_call" | custom-call | flops 1610612736 | bytes 884736 | tf_op jit(solution)/shard_map/cond/branch_1_fun/pallas_call | solution.py:249
  26.8 0.0 collective-permute-done.12
  26.9 0.4 collective-permute-start.19
  27.3 0.2 collective-permute-start.17
  27.5 1.1 %collective-permute-done.19.refs_6_ = bf16[2,128,768]{2,1,0:T(8,128)(2,1)S(1)} collective-permute-done((bf16[2,128,768]{2,1,0:T(8,128)(2,1)S(1)}, bf16[2,128,768]{2,1,0:T(8,128)(2,1)S(1)}, u32[]{:S(2)}, u32[]{:S(2)}) %collective-permute-start.19) | collective-permute-done | bytes 393248 | tf_op jit(solution)/shard_map/cond/branch_1_fun/ppermute | solution.py:27
  28.6 0.4 collective-permute-start.20
  29.0 2.9 %branch_1_fun.5.refs_2_ = f32[2048,256]{1,0:T(8,128)S(1)} custom-call(f32[64,768]{1,0:T(8,128)S(1)} %copy-done.15, f32[64,768]{1,0:T(8,128)S(1)} %copy-done.11, f32[2048,256]{1,0:T(8,128)S(1)} %get-tuple-element.165.refs_2_, bf16[1,32,1536]{2,1,0:T(8,128)(2,1)S(1)} %get-tuple-element.254.refs_4_.refs_3_, ...), custom_call_target="tpu_custom_call" | custom-call | flops 1610612736 | bytes 884736 | tf_op jit(solution)/shard_map/cond/branch_1_fun/pallas_call | solution.py:249
  31.9 6.0 %collective-permute-done.17.refs_7_ = bf16[2,128,768]{2,1,0:T(8,128)(2,1)S(1)} collective-permute-done((bf16[2,128,768]{2,1,0:T(8,128)(2,1)S(1)}, bf16[2,128,768]{2,1,0:T(8,128)(2,1)S(1)}, u32[]{:S(2)}, u32[]{:S(2)}) %collective-permute-start.17) | collective-permute-done | bytes 393248 | tf_op jit(solution)/shard_map/cond/branch_1_fun/ppermute | solution.py:27
  37.9 0.9 %collective-permute-start.21 = (bf16[2,128,768]{2,1,0:T(8,128)(2,1)S(1)}, bf16[2,128,768]{2,1,0:T(8,128)(2,1)S(1)}, u32[]{:S(2)}, u32[]{:S(2)}) collective-permute-start(bf16[2,128,768]{2,1,0:T(8,128)(2,1)S(1)} %collective-permute-done.17.refs_7_), channel_id=1, source_target_pairs={{0,1},{1,0},{2,3},{3,2},{4,5},{5,4},{6,7},{7,6},{8,9},{9,8},{10,11... | collective-permute-start | bytes 1179656 | tf_op jit(solution)/shard_map/cond/branch_1_fun/ppermute | solution.py:27
  38.8 2.9 %branch_1_fun.6.refs_2_ = f32[2048,256]{1,0:T(8,128)S(1)} custom-call(f32[64,768]{1,0:T(8,128)S(1)} %copy-done.15, f32[64,768]{1,0:T(8,128)S(1)} %copy-done.11, f32[2048,256]{1,0:T(8,128)S(1)} %branch_1_fun.5.refs_2_, bf16[1,32,1536]{2,1,0:T(8,128)(2,1)S(1)} %get-tuple-element.251.refs_3_.refs_5_, ...), custom_call_target="tpu_custom_call" | custom-call | flops 1610612736 | bytes 884736 | tf_op jit(solution)/shard_map/cond/branch_1_fun/pallas_call | solution.py:249
  41.7 3.8 %branch_1_fun.7 = bf16[2,32,8192]{2,1,0:T(8,128)(2,1)S(1)} custom-call(f32[64,768]{1,0:T(8,128)S(1)} %copy-done.15, f32[64,768]{1,0:T(8,128)S(1)} %copy-done.11, f32[2048,256]{1,0:T(8,128)S(1)} %branch_1_fun.6.refs_2_, f32[2,32,128]{2,1,0:T(8,128)S(1)} %get-tuple-element.170.refs_3_, s32[2,8]{1,0:T(2,128)S(1)} %copy-done.6, ...), custom_call_target="tpu_custom_call" | custom-call | flops 1610612736 | bytes 884736 | tf_op jit(solution)/shard_map/cond/branch_1_fun/pallas_call | solution.py:249
  45.8 0.0 copy-start.9
  45.8 1.0 %copy-done.9 = bf16[2,32,8192]{2,1,0:T(8,128)(2,1)} copy-done((bf16[2,32,8192]{2,1,0:T(8,128)(2,1)}, bf16[2,32,8192]{2,1,0:T(8,128)(2,1)S(1)}, u32[]{:S(2)}) %copy-start.9) | copy-done | bytes 1048600
  (19 shorter events, 0.2 us)
Async XLA Ops:
  0.0 1.0 %copy-start = (bf16[1,128,1536]{2,1,0:T(8,128)(2,1)S(1)}, bf16[1,128,1536]{2,1,0:T(8,128)(2,1)}, u32[]{:S(2)}) copy-start(bf16[1,128,1536]{2,1,0:T(8,128)(2,1)} %spectra_ref.1) | copy-start | bytes 1179652
  3.1 19.9 %copy-start.2 = (s32[4,1024]{1,0:T(4,128)S(1)}, s32[4,1024]{1,0:T(4,128)}, u32[]{:S(2)}) copy-start(s32[4,1024]{1,0:T(4,128)} %get-tuple-element.152.refs_2_) | copy-start | bytes 49156 | tf_op jit(solution)/shard_map/cond
  3.2 19.9 %copy-start.6 = (s32[2,8]{1,0:T(2,128)S(1)}, s32[2,8]{1,0:T(2,128)}, u32[]{:S(2)}) copy-start(s32[2,8]{1,0:T(2,128)} %get-tuple-element.153.refs_3_.refs_4_) | copy-start | bytes 196 | tf_op jit(solution)/shard_map/cond
  3.2 19.9 %copy-start.11 = (f32[64,768]{1,0:T(8,128)S(1)}, f32[64,768]{1,0:T(8,128)}, u32[]{:S(2)}) copy-start(f32[64,768]{1,0:T(8,128)} %get-tuple-element.144.refs_1_) | copy-start | bytes 589828 | tf_op jit(solution)/shard_map/cond
  3.2 19.9 %copy-start.15 = (f32[64,768]{1,0:T(8,128)S(1)}, f32[64,768]{1,0:T(8,128)}, u32[]{:S(2)}) copy-start(f32[64,768]{1,0:T(8,128)} %get-tuple-element.143.refs_0_) | copy-start | bytes 589828 | tf_op jit(solution)/shard_map/cond
  3.2 11.1 %collective-permute-start.15 = (bf16[1,128,768]{2,1,0:T(8,128)(2,1)S(1)}, bf16[1,128,768]{2,1,0:T(8,128)(2,1)S(1)}, u32[]{:S(2)}, u32[]{:S(2)}) collective-permute-start(bf16[1,128,768]{2,1,0:T(8,128)(2,1)S(1)} %get-tuple-element.155), channel_id=1, source_target_pairs={{0,24},{4,28},{8,16},{12,20},{16,8},{20,12},{24,0},{28,4},{1,25},{... | collective-permute-start | bytes 589832 | tf_op jit(solution)/shard_map/cond/branch_1_fun/ppermute | solution.py:27
  3.4 10.9 %collective-permute-start.14 = (bf16[1,128,768]{2,1,0:T(8,128)(2,1)S(1)}, bf16[1,128,768]{2,1,0:T(8,128)(2,1)S(1)}, u32[]{:S(2)}, u32[]{:S(2)}) collective-permute-start(bf16[1,128,768]{2,1,0:T(8,128)(2,1)S(1)} %get-tuple-element.155), channel_id=1, source_target_pairs={{0,4},{4,0},{8,12},{12,8},{16,20},{20,16},{24,28},{28,24},{1,5},{5... | collective-permute-start | bytes 589832 | tf_op jit(solution)/shard_map/cond/branch_1_fun/ppermute | solution.py:27
  4.7 5.2 %collective-permute-start.10 = (bf16[1,64,1536]{2,1,0:T(8,128)(2,1)S(1)}, bf16[1,64,1536]{2,1,0:T(8,128)(2,1)S(1)}, u32[]{:S(2)}, u32[]{:S(2)}) collective-permute-start(bf16[1,64,1536]{2,1,0:T(8,128)(2,1)S(1)} %get-tuple-element.248), channel_id=1, source_target_pairs={{0,2},{1,3},{2,0},{3,1},{4,6},{5,7},{6,4},{7,5},{8,10},{9,11},{10,... | collective-permute-start | bytes 589832 | tf_op jit(solution)/shard_map/cond/branch_1_fun/ppermute | solution.py:27
  9.9 16.9 %collective-permute-start.12 = (bf16[1,128,768]{2,1,0:T(8,128)(2,1)S(1)}, bf16[1,128,768]{2,1,0:T(8,128)(2,1)S(1)}, u32[]{:S(2)}, u32[]{:S(2)}) collective-permute-start(bf16[1,128,768]{2,1,0:T(8,128)(2,1)S(1)} %get-tuple-element.149), channel_id=1, source_target_pairs={{0,24},{4,28},{8,16},{12,20},{16,8},{20,12},{24,0},{28,4},{1,25},{... | collective-permute-start | bytes 589832 | tf_op jit(solution)/shard_map/cond/branch_1_fun/ppermute | solution.py:27
  11.2 15.6 %collective-permute-start.11 = (bf16[1,128,768]{2,1,0:T(8,128)(2,1)S(1)}, bf16[1,128,768]{2,1,0:T(8,128)(2,1)S(1)}, u32[]{:S(2)}, u32[]{:S(2)}) collective-permute-start(bf16[1,128,768]{2,1,0:T(8,128)(2,1)S(1)} %get-tuple-element.149), channel_id=1, source_target_pairs={{0,4},{4,0},{8,12},{12,8},{16,20},{20,16},{24,28},{28,24},{1,5},{5... | collective-permute-start | bytes 589832 | tf_op jit(solution)/shard_map/cond/branch_1_fun/ppermute | solution.py:27
  11.5 10.2 %collective-permute-start.13 = (bf16[2,32,1536]{2,1,0:T(8,128)(2,1)S(1)}, bf16[2,32,1536]{2,1,0:T(8,128)(2,1)S(1)}, u32[]{:S(2)}, u32[]{:S(2)}) collective-permute-start(bf16[2,32,1536]{2,1,0:T(8,128)(2,1)S(1)} %pad_maximum_fusion.1), channel_id=1, source_target_pairs={{0,1},{1,0},{2,3},{3,2},{4,5},{5,4},{6,7},{7,6},{8,9},{9,8},{10,11... | collective-permute-start | bytes 589832 | tf_op jit(solution)/shard_map/cond/branch_1_fun/ppermute | solution.py:27
  14.3 13.2 %collective-permute-start.18 = (bf16[2,128,768]{2,1,0:T(8,128)(2,1)S(1)}, bf16[2,128,768]{2,1,0:T(8,128)(2,1)S(1)}, u32[]{:S(2)}, u32[]{:S(2)}) collective-permute-start(bf16[2,128,768]{2,1,0:T(8,128)(2,1)S(1)} %constant_dynamic-update-slice_fusion.4.refs_6_), channel_id=1, source_target_pairs={{0,2},{1,3},{2,0},{3,1},{4,6},{5,7},{6,4},{7,5},{8,10},{9,11},{10,... | collective-permute-start | bytes 1179656 | tf_op jit(solution)/shard_map/cond/branch_1_fun/ppermute | solution.py:27
  15.6 7.5 %collective-permute-start.16 = (bf16[2,128,768]{2,1,0:T(8,128)(2,1)S(1)}, bf16[2,128,768]{2,1,0:T(8,128)(2,1)S(1)}, u32[]{:S(2)}, u32[]{:S(2)}) collective-permute-start(bf16[2,128,768]{2,1,0:T(8,128)(2,1)S(1)} %constant_dynamic-update-slice_fusion.4.refs_6_), channel_id=1, source_target_pairs={{0,1},{1,0},{2,3},{3,2},{4,5},{5,4},{6,7},{7,6},{8,9},{9,8},{10,11... | collective-permute-start | bytes 1179656 | tf_op jit(solution)/shard_map/cond/branch_1_fun/ppermute | solution.py:27
  26.9 1.8 %collective-permute-start.19 = (bf16[2,128,768]{2,1,0:T(8,128)(2,1)S(1)}, bf16[2,128,768]{2,1,0:T(8,128)(2,1)S(1)}, u32[]{:S(2)}, u32[]{:S(2)}) collective-permute-start(bf16[2,128,768]{2,1,0:T(8,128)(2,1)S(1)} %constant_dynamic-update-slice_fusion.6.refs_5_), channel_id=1, source_target_pairs={{0,1},{1,0},{2,3},{3,2},{4,5},{5,4},{6,7},{7,6},{8,9},{9,8},{10,11... | collective-permute-start | bytes 1179656 | tf_op jit(solution)/shard_map/cond/branch_1_fun/ppermute | solution.py:27
  27.3 10.6 %collective-permute-start.17 = (bf16[2,128,768]{2,1,0:T(8,128)(2,1)S(1)}, bf16[2,128,768]{2,1,0:T(8,128)(2,1)S(1)}, u32[]{:S(2)}, u32[]{:S(2)}) collective-permute-start(bf16[2,128,768]{2,1,0:T(8,128)(2,1)S(1)} %constant_dynamic-update-slice_fusion.6.refs_5_), channel_id=1, source_target_pairs={{0,2},{1,3},{2,0},{3,1},{4,6},{5,7},{6,4},{7,5},{8,10},{9,11},{10,... | collective-permute-start | bytes 1179656 | tf_op jit(solution)/shard_map/cond/branch_1_fun/ppermute | solution.py:27
  28.6 9.2 %collective-permute-start.20 = (bf16[2,128,768]{2,1,0:T(8,128)(2,1)S(1)}, bf16[2,128,768]{2,1,0:T(8,128)(2,1)S(1)}, u32[]{:S(2)}, u32[]{:S(2)}) collective-permute-start(bf16[2,128,768]{2,1,0:T(8,128)(2,1)S(1)} %collective-permute-done.18.refs_5_), channel_id=1, source_target_pairs={{0,1},{1,0},{2,3},{3,2},{4,5},{5,4},{6,7},{7,6},{8,9},{9,8},{10,11... | collective-permute-start | bytes 1179656 | tf_op jit(solution)/shard_map/cond/branch_1_fun/ppermute | solution.py:27
  37.9 3.9 %collective-permute-start.21 = (bf16[2,128,768]{2,1,0:T(8,128)(2,1)S(1)}, bf16[2,128,768]{2,1,0:T(8,128)(2,1)S(1)}, u32[]{:S(2)}, u32[]{:S(2)}) collective-permute-start(bf16[2,128,768]{2,1,0:T(8,128)(2,1)S(1)} %collective-permute-done.17.refs_7_), channel_id=1, source_target_pairs={{0,1},{1,0},{2,3},{3,2},{4,5},{5,4},{6,7},{7,6},{8,9},{9,8},{10,11... | collective-permute-start | bytes 1179656 | tf_op jit(solution)/shard_map/cond/branch_1_fun/ppermute | solution.py:27
  45.8 1.0 %copy-start.9 = (bf16[2,32,8192]{2,1,0:T(8,128)(2,1)}, bf16[2,32,8192]{2,1,0:T(8,128)(2,1)S(1)}, u32[]{:S(2)}) copy-start(bf16[2,32,8192]{2,1,0:T(8,128)(2,1)S(1)} %get-tuple-element.367) | copy-start | bytes 3145732

commit v2 on v1

--- a/solution.py
+++ b/solution.py
@@ -12,6 +12,7 @@
 LAGS = 64
 ROUNDS = 2
 LAG_STEP = 16
+LAST_LAG_STEP = 32
 BIN_STEP = 256
 PARTS = 2
 SWITCH_BLOCKS = 8
@@ -110,6 +111,7 @@
 
 def correlate_kernel(plan, shift, first, last, *refs):
     refs = list(refs)
+    lag_step = LAST_LAG_STEP if last else LAG_STEP
     take = lambda count: [refs.pop(0) for _ in range(count)]
     cos_ref, sin_ref = take(2)
     if first:
@@ -153,7 +155,7 @@
         scales = [scale_ref[r] for r in rounds]
 
     def one_step(index, carry):
-        step = pl.multiple_of(index * LAG_STEP, LAG_STEP)
+        step = pl.multiple_of(index * lag_step, lag_step)
         total = None
         for n, (own_at, first_bin, width) in enumerate(plan):
             for q in range(w_count):
@@ -162,10 +164,10 @@
                     b = first_bin + c
                     real = own_refs[own_at][q, :, b : b + size]
                     imag = own_refs[own_at][q, :, bins + b : bins + b + size]
-                    cosine = cos_ref[pl.ds(step, LAG_STEP), b : b + size].astype(jnp.bfloat16)
-                    sine = sin_ref[pl.ds(step, LAG_STEP), b : b + size].astype(jnp.bfloat16)
+                    cosine = cos_ref[pl.ds(step, lag_step), b : b + size].astype(jnp.bfloat16)
+                    sine = sin_ref[pl.ds(step, lag_step), b : b + size].astype(jnp.bfloat16)
                     turned = [[], []]
-                    for t in range(LAG_STEP):
+                    for t in range(lag_step):
                         cos, sin = cosine[t : t + 1], sine[t : t + 1]
                         turned[0].append(real * cos - imag * sin)
                         turned[1].append(real * sin + imag * cos)
@@ -180,13 +182,13 @@
                         )
                         term = dot(jnp.concatenate(turned[side], axis=0), rhs)
                         total = term if total is None else total + term
-        at = pl.ds(pl.multiple_of(step * rows, LAG_STEP * rows), LAG_STEP * rows)
+        at = pl.ds(pl.multiple_of(step * rows, lag_step * rows), lag_step * rows)
         if not first:
             total = total + total_ref[at, :]
         if not last:
             out_ref[at, :] = total
             return carry
-        for t in range(LAG_STEP):
+        for t in range(lag_step):
             lanes = pl.ds(pl.multiple_of((step + t) * block, block), block)
             for side in range(ROUNDS):
                 part = total[t * rows : (t + 1) * rows, side * block : (side + 1) * block]
@@ -195,15 +197,15 @@
         return carry
 
     def copy(index):
-        size = LAG_STEP * block
+        size = lag_step * block
         lanes = pl.ds(pl.multiple_of(index * size, size), size)
         return pltpu.make_async_copy(
             stage_ref.at[:, :, lanes], out_ref.at[:, :, lanes], copy_sems.at[index]
         )
 
-    lax.fori_loop(0, LAGS // LAG_STEP, one_step, 0)
-    if last:
-        for index in range(LAGS // LAG_STEP):
+    lax.fori_loop(0, LAGS // lag_step, one_step, 0)
+    if last:
+        for index in range(LAGS // lag_step):
             copy(index).wait()
 
 
@@ -238,7 +240,7 @@
         outs, out_specs = [final], [pl.BlockSpec(memory_space=pl.ANY)]
         scratch = [
             pltpu.VMEM(final.shape, final.dtype),
-            pltpu.SemaphoreType.DMA((LAGS // LAG_STEP,)),
+            pltpu.SemaphoreType.DMA((LAGS // LAST_LAG_STEP,)),
         ]
     elif first:
         outs, out_specs = [running, shape((ROUNDS, rows, block), jnp.float32)], [VMEM] * 2
@@ -283,14 +285,19 @@
                 held[d, n] = flip(before, "win", bit)
         return held[d, n], state
 
+    early = set()
     for number, (d, n) in enumerate(steps):
         here, state = stack(d, n, state)
         across = flip(here, "win", low)
+        pieces = [] if (d, n) in early else [(own[d], n * width, here)]
         ahead = number + 1
         if 0 < number and ahead < len(steps) and steps[ahead][0] != 0:
             coming, state = stack(*steps[ahead], state)
-            (held[steps[ahead]], across), state = after((coming, across), state)
-        pieces = [(own[d], n * width, here), (own[d | low], n * width, across)]
+            (coming, across), state = after((coming, across), state)
+            held[steps[ahead]] = coming
+            early.add(steps[ahead])
+            pieces.append((own[steps[ahead][0]], steps[ahead][1] * width, coming))
+        pieces.append((own[d | low], n * width, across))
         state = correlate(state, masks, matching, shift, pieces, ahead == len(steps))
     return state
 

time: 47 us -> 45.4 us (0.966)
  the two profiles are of different devices: /device:TPU:17 before, /device:TPU:1 now
where the time goes in v2:
time: 45.4 us; the launch traced here: 45.2 us
  starting transfers between devices  15.9 us (35%)
  Pallas kernels  14.2 us (31%)
  waiting for transfers between devices  11.8 us (26%)
  local copies, waits for them, and re-layouts  2.06 us (5%)
  between operations  0.68 us (1%)
  loops' own time  0.57 us (1%)
    ppermute x12, starting transfers between devices, flip(): lax.ppermute(value, axis, [(i, i ^ bits) for i in range(lax.axis_size(axi...  15.9 us
    pallas_call x4, Pallas kernels, correlate(): pl.pallas_call(functools.partial(correlate_kernel, plan, shift, first, la...  12.7 us
    ppermute x12, waiting for transfers between devices, flip(): lax.ppermute(value, axis, [(i, i ^ bits) for i in range(lax.axis_size(axi...  11.8 us
    unnamed x4, local copies, waits for them, and re-layouts  1.96 us
    pallas_call x1, Pallas kernels, prepare(): pl.pallas_call(prepare_kernel, out_shape=[shape(spectra.shape, jnp.bfloat...  1.46 us
  transfers between devices with their start and end apart: 12, of which 5 were waited for; matrix products, arithmetic and copies ran while one was open for 0% of the time, Pallas kernels for 23%

profile of v2, /device:TPU:1, one launch (start us, length us, event | category | flops | bytes accessed | tf_op | source)
XLA Modules:
  0.0 45.2 jit_solution(3906833320857896499)
XLA Ops:
  0.0 1.0 %copy-done = bf16[1,128,1536]{2,1,0:T(8,128)(2,1)S(1)} copy-done((bf16[1,128,1536]{2,1,0:T(8,128)(2,1)S(1)}, bf16[1,128,1536]{2,1,0:T(8,128)(2,1)}, u32[]{:S(2)}) %copy-start) | copy-done | bytes 393240
  1.0 1.5 %shard_map.329 = (bf16[1,128,1536]{2,1,0:T(8,128)(2,1)S(1)}, bf16[1,128,768]{2,1,0:T(8,128)(2,1)S(1)}, bf16[1,128,768]{2,1,0:T(8,128)(2,1)S(1)}, s32[1]{0:T(128)}) custom-call(bf16[1,128,1536]{2,1,0:T(8,128)(2,1)S(1)} %copy-done, s32[4,1024]{1,0:T(4,128)} %masks_ref.1, s32[2,8]{1,0:T(2,128)} %matching_ref.1), custom_call_target="tpu_custom_call" | custom-call | tf_op jit(solution)/shard_map/pallas_call | solution.py:102
  3.1 41.1 %conditional.1 = (bf16[2,32,8192]{2,1,0:T(8,128)(2,1)S(1)}) conditional(s32[]{:T(128)} %bitcast, (bf16[1,128,1536]{2,1,0:T(8,128)(2,1)S(1)}, bf16[1,128,768]{2,1,0:T(8,128)(2,1)S(1)}, bf16[1,128,768]{2,1,0:T(8,128)(2,1)S(1)}, f32[64,768]{1,0:T(8,128)}, f32[64,768]{1,0:T(8,128)}, /*index=5*/s32[4,1024]{1,0:T(4,128)}, ...), branch_computations={%region_0.1_spmd, %region_1.2_spmd, %region_2.3_spmd, %region_3.4_... | conditional | flops 6442942464 | bytes 23266200 | solution.py:329
  3.3 0.0 copy-start.3
  3.3 0.0 copy-start.7
  3.3 0.0 copy-start.12
  3.4 0.0 copy-start.16
  3.4 4.2 %collective-permute-start.27 = (bf16[1,128,768]{2,1,0:T(8,128)(2,1)S(1)}, bf16[1,128,768]{2,1,0:T(8,128)(2,1)S(1)}, u32[]{:S(2)}, u32[]{:S(2)}) collective-permute-start(bf16[1,128,768]{2,1,0:T(8,128)(2,1)S(1)} %get-tuple-element.184), channel_id=1, source_target_pairs={{0,20},{4,16},{8,28},{12,24},{16,4},{20,0},{24,12},{28,8},{1,21},{... | collective-permute-start | bytes 589832 | tf_op jit(solution)/shard_map/cond/branch_2_fun/ppermute | solution.py:28
  7.5 1.3 %collective-permute-start.26 = (bf16[1,128,768]{2,1,0:T(8,128)(2,1)S(1)}, bf16[1,128,768]{2,1,0:T(8,128)(2,1)S(1)}, u32[]{:S(2)}, u32[]{:S(2)}) collective-permute-start(bf16[1,128,768]{2,1,0:T(8,128)(2,1)S(1)} %get-tuple-element.184), channel_id=1, source_target_pairs={{0,8},{4,12},{8,0},{12,4},{16,24},{20,28},{24,16},{28,20},{1,9},{5... | collective-permute-start | bytes 589832 | tf_op jit(solution)/shard_map/cond/branch_2_fun/ppermute | solution.py:28
  8.9 1.3 %collective-permute-start.22 = (bf16[1,64,1536]{2,1,0:T(8,128)(2,1)S(1)}, bf16[1,64,1536]{2,1,0:T(8,128)(2,1)S(1)}, u32[]{:S(2)}, u32[]{:S(2)}) collective-permute-start(bf16[1,64,1536]{2,1,0:T(8,128)(2,1)S(1)} %get-tuple-element.256), channel_id=1, source_target_pairs={{0,2},{1,3},{2,0},{3,1},{4,6},{5,7},{6,4},{7,5},{8,10},{9,11},{10,... | collective-permute-start | bytes 589832 | tf_op jit(solution)/shard_map/cond/branch_2_fun/ppermute | solution.py:28
  10.2 3.9 %collective-permute-done.22 = bf16[1,64,1536]{2,1,0:T(8,128)(2,1)S(1)} collective-permute-done((bf16[1,64,1536]{2,1,0:T(8,128)(2,1)S(1)}, bf16[1,64,1536]{2,1,0:T(8,128)(2,1)S(1)}, u32[]{:S(2)}, u32[]{:S(2)}) %collective-permute-start.22) | collective-permute-done | bytes 196640 | tf_op jit(solution)/shard_map/cond/branch_2_fun/ppermute | solution.py:28
  14.1 0.2 collective-permute-start.24
  14.2 0.4 collective-permute-start.23
  14.7 2.5 %collective-permute-start.25 = (bf16[2,32,1536]{2,1,0:T(8,128)(2,1)S(1)}, bf16[2,32,1536]{2,1,0:T(8,128)(2,1)S(1)}, u32[]{:S(2)}, u32[]{:S(2)}) collective-permute-start(bf16[2,32,1536]{2,1,0:T(8,128)(2,1)S(1)} %pad_maximum_fusion.2), channel_id=1, source_target_pairs={{0,1},{1,0},{2,3},{3,2},{4,5},{5,4},{6,7},{7,6},{8,9},{9,8},{10,11... | collective-permute-start | bytes 589832 | tf_op jit(solution)/shard_map/cond/branch_2_fun/ppermute | solution.py:28
  17.2 1.3 %collective-permute-start.30 = (bf16[2,128,768]{2,1,0:T(8,128)(2,1)S(1)}, bf16[2,128,768]{2,1,0:T(8,128)(2,1)S(1)}, u32[]{:S(2)}, u32[]{:S(2)}) collective-permute-start(bf16[2,128,768]{2,1,0:T(8,128)(2,1)S(1)} %constant_dynamic-update-slice_fusion.8.refs_6_), channel_id=1, source_target_pairs={{0,2},{1,3},{2,0},{3,1},{4,6},{5,7},{6,4},{7,5},{8,10},{9,11},{10,... | collective-permute-start | bytes 1179656 | tf_op jit(solution)/shard_map/cond/branch_2_fun/ppermute | solution.py:28
  18.5 1.2 %collective-permute-start.28 = (bf16[2,128,768]{2,1,0:T(8,128)(2,1)S(1)}, bf16[2,128,768]{2,1,0:T(8,128)(2,1)S(1)}, u32[]{:S(2)}, u32[]{:S(2)}) collective-permute-start(bf16[2,128,768]{2,1,0:T(8,128)(2,1)S(1)} %constant_dynamic-update-slice_fusion.8.refs_6_), channel_id=1, source_target_pairs={{0,1},{1,0},{2,3},{3,2},{4,5},{5,4},{6,7},{7,6},{8,9},{9,8},{10,11... | collective-permute-start | bytes 1179656 | tf_op jit(solution)/shard_map/cond/branch_2_fun/ppermute | solution.py:28
  19.8 1.3 %collective-permute-done.28.refs_7_ = bf16[2,128,768]{2,1,0:T(8,128)(2,1)S(1)} collective-permute-done((bf16[2,128,768]{2,1,0:T(8,128)(2,1)S(1)}, bf16[2,128,768]{2,1,0:T(8,128)(2,1)S(1)}, u32[]{:S(2)}, u32[]{:S(2)}) %collective-permute-start.28) | collective-permute-done | bytes 393248 | tf_op jit(solution)/shard_map/cond/branch_2_fun/ppermute | solution.py:28
  21.1 3.7 %branch_2_fun.4 = (f32[2048,256]{1,0:T(8,128)S(1)}, f32[2,32,128]{2,1,0:T(8,128)S(1)}) custom-call(f32[64,768]{1,0:T(8,128)S(1)} %copy-done.7, f32[64,768]{1,0:T(8,128)S(1)} %copy-done.3, s32[4,1024]{1,0:T(4,128)S(1)} %copy-done.16, s32[2,8]{1,0:T(2,128)S(1)} %copy-done.12, bf16[1,32,1536]{2,1,0:T(8,128)(2,1)S(1)} %get-tuple-element.262.refs_4_.refs_3_, ...), custom_call_target="tpu_custom_call" | custom-call | flops 1610612736 | bytes 884736 | tf_op jit(solution)/shard_map/cond/branch_2_fun/pallas_call | solution.py:251
  24.8 1.4 %collective-permute-done.24 = bf16[1,128,768]{2,1,0:T(8,128)(2,1)S(1)} collective-permute-done((bf16[1,128,768]{2,1,0:T(8,128)(2,1)S(1)}, bf16[1,128,768]{2,1,0:T(8,128)(2,1)S(1)}, u32[]{:S(2)}, u32[]{:S(2)}) %collective-permute-start.24) | collective-permute-done | bytes 196640 | tf_op jit(solution)/shard_map/cond/branch_2_fun/ppermute | solution.py:28
  26.3 1.1 %collective-permute-start.31 = (bf16[2,128,768]{2,1,0:T(8,128)(2,1)S(1)}, bf16[2,128,768]{2,1,0:T(8,128)(2,1)S(1)}, u32[]{:S(2)}, u32[]{:S(2)}) collective-permute-start(bf16[2,128,768]{2,1,0:T(8,128)(2,1)S(1)} %constant_dynamic-update-slice_fusion.10.refs_6_), channel_id=1, source_target_pairs={{0,1},{1,0},{2,3},{3,2},{4,5},{5,4},{6,7},{7,6},{8,9},{9,8},{10,11... | collective-permute-start | bytes 1179656 | tf_op jit(solution)/shard_map/cond/branch_2_fun/ppermute | solution.py:28
  27.4 1.2 %collective-permute-start.29 = (bf16[2,128,768]{2,1,0:T(8,128)(2,1)S(1)}, bf16[2,128,768]{2,1,0:T(8,128)(2,1)S(1)}, u32[]{:S(2)}, u32[]{:S(2)}) collective-permute-start(bf16[2,128,768]{2,1,0:T(8,128)(2,1)S(1)} %constant_dynamic-update-slice_fusion.10.refs_6_), channel_id=1, source_target_pairs={{0,2},{1,3},{2,0},{3,1},{4,6},{5,7},{6,4},{7,5},{8,10},{9,11},{10,... | collective-permute-start | bytes 1179656 | tf_op jit(solution)/shard_map/cond/branch_2_fun/ppermute | solution.py:28
  28.6 0.0 collective-permute-done.30.refs_7_
  28.6 0.1 collective-permute-done.31.refs_8_
  28.8 0.4 collective-permute-start.32
  29.1 4.0 %branch_2_fun.5.refs_2_ = f32[2048,256]{1,0:T(8,128)S(1)} custom-call(f32[64,768]{1,0:T(8,128)S(1)} %copy-done.7, f32[64,768]{1,0:T(8,128)S(1)} %copy-done.3, f32[2048,256]{1,0:T(8,128)S(1)} %get-tuple-element.194.refs_2_, bf16[1,32,1536]{2,1,0:T(8,128)(2,1)S(1)} %get-tuple-element.262.refs_4_.refs_3_, ...), custom_call_target="tpu_custom_call" | custom-call | flops 2415919104 | bytes 1327104 | tf_op jit(solution)/shard_map/cond/branch_2_fun/pallas_call | solution.py:251
  33.1 5.0 %collective-permute-done.29.refs_5_ = bf16[2,128,768]{2,1,0:T(8,128)(2,1)S(1)} collective-permute-done((bf16[2,128,768]{2,1,0:T(8,128)(2,1)S(1)}, bf16[2,128,768]{2,1,0:T(8,128)(2,1)S(1)}, u32[]{:S(2)}, u32[]{:S(2)}) %collective-permute-start.29) | collective-permute-done | bytes 393248 | tf_op jit(solution)/shard_map/cond/branch_2_fun/ppermute | solution.py:28
  38.1 0.0 collective-permute-done.32.refs_6_
  38.1 0.9 %collective-permute-start.33 = (bf16[2,128,768]{2,1,0:T(8,128)(2,1)S(1)}, bf16[2,128,768]{2,1,0:T(8,128)(2,1)S(1)}, u32[]{:S(2)}, u32[]{:S(2)}) collective-permute-start(bf16[2,128,768]{2,1,0:T(8,128)(2,1)S(1)} %collective-permute-done.29.refs_5_), channel_id=1, source_target_pairs={{0,1},{1,0},{2,3},{3,2},{4,5},{5,4},{6,7},{7,6},{8,9},{9,8},{10,11... | collective-permute-start | bytes 1179656 | tf_op jit(solution)/shard_map/cond/branch_2_fun/ppermute | solution.py:28
  39.0 2.9 %branch_2_fun.6.refs_2_ = f32[2048,256]{1,0:T(8,128)S(1)} custom-call(f32[64,768]{1,0:T(8,128)S(1)} %copy-done.7, f32[64,768]{1,0:T(8,128)S(1)} %copy-done.3, f32[2048,256]{1,0:T(8,128)S(1)} %branch_2_fun.5.refs_2_, bf16[1,32,1536]{2,1,0:T(8,128)(2,1)S(1)} %get-tuple-element.259.refs_4_.refs_3_, bf16[1,32,1536]{2,1,0:T(8,128)(2,1)S(1)} %get-tuple-element.257.refs_4_.refs_5_, ...), custom_call_target="tpu_custom_call" | custom-call | flops 1610612736 | bytes 884736 | tf_op jit(solution)/shard_map/cond/branch_2_fun/pallas_call | solution.py:251
  41.9 2.1 %branch_2_fun.7 = bf16[2,32,8192]{2,1,0:T(8,128)(2,1)S(1)} custom-call(f32[64,768]{1,0:T(8,128)S(1)} %copy-done.7, f32[64,768]{1,0:T(8,128)S(1)} %copy-done.3, f32[2048,256]{1,0:T(8,128)S(1)} %branch_2_fun.6.refs_2_, f32[2,32,128]{2,1,0:T(8,128)S(1)} %get-tuple-element.200.refs_3_, s32[2,8]{1,0:T(2,128)S(1)} %copy-done.12, ...), custom_call_target="tpu_custom_call" | custom-call | flops 805306368 | bytes 442368 | tf_op jit(solution)/shard_map/cond/branch_2_fun/pallas_call | solution.py:251
  44.2 0.0 copy-start.9
  44.2 1.0 %copy-done.9 = bf16[2,32,8192]{2,1,0:T(8,128)(2,1)} copy-done((bf16[2,32,8192]{2,1,0:T(8,128)(2,1)}, bf16[2,32,8192]{2,1,0:T(8,128)(2,1)S(1)}, u32[]{:S(2)}) %copy-start.9) | copy-done | bytes 1048600
  (19 shorter events, 0.2 us)
Async XLA Ops:
  0.0 1.0 %copy-start = (bf16[1,128,1536]{2,1,0:T(8,128)(2,1)S(1)}, bf16[1,128,1536]{2,1,0:T(8,128)(2,1)}, u32[]{:S(2)}) copy-start(bf16[1,128,1536]{2,1,0:T(8,128)(2,1)} %spectra_ref.1) | copy-start | bytes 1179652
  3.3 17.8 %copy-start.3 = (f32[64,768]{1,0:T(8,128)S(1)}, f32[64,768]{1,0:T(8,128)}, u32[]{:S(2)}) copy-start(f32[64,768]{1,0:T(8,128)} %get-tuple-element.173.refs_1_) | copy-start | bytes 589828 | tf_op jit(solution)/shard_map/cond
  3.3 17.8 %copy-start.7 = (f32[64,768]{1,0:T(8,128)S(1)}, f32[64,768]{1,0:T(8,128)}, u32[]{:S(2)}) copy-start(f32[64,768]{1,0:T(8,128)} %get-tuple-element.172.refs_0_) | copy-start | bytes 589828 | tf_op jit(solution)/shard_map/cond
  3.3 17.7 %copy-start.12 = (s32[2,8]{1,0:T(2,128)S(1)}, s32[2,8]{1,0:T(2,128)}, u32[]{:S(2)}) copy-start(s32[2,8]{1,0:T(2,128)} %get-tuple-element.182.refs_3_.refs_4_) | copy-start | bytes 196 | tf_op jit(solution)/shard_map/cond
  3.4 17.7 %copy-start.16 = (s32[4,1024]{1,0:T(4,128)S(1)}, s32[4,1024]{1,0:T(4,128)}, u32[]{:S(2)}) copy-start(s32[4,1024]{1,0:T(4,128)} %get-tuple-element.181.refs_2_) | copy-start | bytes 49156 | tf_op jit(solution)/shard_map/cond
  3.4 13.8 %collective-permute-start.27 = (bf16[1,128,768]{2,1,0:T(8,128)(2,1)S(1)}, bf16[1,128,768]{2,1,0:T(8,128)(2,1)S(1)}, u32[]{:S(2)}, u32[]{:S(2)}) collective-permute-start(bf16[1,128,768]{2,1,0:T(8,128)(2,1)S(1)} %get-tuple-element.184), channel_id=1, source_target_pairs={{0,20},{4,16},{8,28},{12,24},{16,4},{20,0},{24,12},{28,8},{1,21},{... | collective-permute-start | bytes 589832 | tf_op jit(solution)/shard_map/cond/branch_2_fun/ppermute | solution.py:28
  7.5 9.6 %collective-permute-start.26 = (bf16[1,128,768]{2,1,0:T(8,128)(2,1)S(1)}, bf16[1,128,768]{2,1,0:T(8,128)(2,1)S(1)}, u32[]{:S(2)}, u32[]{:S(2)}) collective-permute-start(bf16[1,128,768]{2,1,0:T(8,128)(2,1)S(1)} %get-tuple-element.184), channel_id=1, source_target_pairs={{0,8},{4,12},{8,0},{12,4},{16,24},{20,28},{24,16},{28,20},{1,9},{5... | collective-permute-start | bytes 589832 | tf_op jit(solution)/shard_map/cond/branch_2_fun/ppermute | solution.py:28
  8.9 5.2 %collective-permute-start.22 = (bf16[1,64,1536]{2,1,0:T(8,128)(2,1)S(1)}, bf16[1,64,1536]{2,1,0:T(8,128)(2,1)S(1)}, u32[]{:S(2)}, u32[]{:S(2)}) collective-permute-start(bf16[1,64,1536]{2,1,0:T(8,128)(2,1)S(1)} %get-tuple-element.256), channel_id=1, source_target_pairs={{0,2},{1,3},{2,0},{3,1},{4,6},{5,7},{6,4},{7,5},{8,10},{9,11},{10,... | collective-permute-start | bytes 589832 | tf_op jit(solution)/shard_map/cond/branch_2_fun/ppermute | solution.py:28
  14.1 12.1 %collective-permute-start.24 = (bf16[1,128,768]{2,1,0:T(8,128)(2,1)S(1)}, bf16[1,128,768]{2,1,0:T(8,128)(2,1)S(1)}, u32[]{:S(2)}, u32[]{:S(2)}) collective-permute-start(bf16[1,128,768]{2,1,0:T(8,128)(2,1)S(1)} %get-tuple-element.178), channel_id=1, source_target_pairs={{0,20},{4,16},{8,28},{12,24},{16,4},{20,0},{24,12},{28,8},{1,21},{... | collective-permute-start | bytes 589832 | tf_op jit(solution)/shard_map/cond/branch_2_fun/ppermute | solution.py:28
  14.2 12.0 %collective-permute-start.23 = (bf16[1,128,768]{2,1,0:T(8,128)(2,1)S(1)}, bf16[1,128,768]{2,1,0:T(8,128)(2,1)S(1)}, u32[]{:S(2)}, u32[]{:S(2)}) collective-permute-start(bf16[1,128,768]{2,1,0:T(8,128)(2,1)S(1)} %get-tuple-element.178), channel_id=1, source_target_pairs={{0,8},{4,12},{8,0},{12,4},{16,24},{20,28},{24,16},{28,20},{1,9},{5... | collective-permute-start | bytes 589832 | tf_op jit(solution)/shard_map/cond/branch_2_fun/ppermute | solution.py:28
  14.7 5.1 %collective-permute-start.25 = (bf16[2,32,1536]{2,1,0:T(8,128)(2,1)S(1)}, bf16[2,32,1536]{2,1,0:T(8,128)(2,1)S(1)}, u32[]{:S(2)}, u32[]{:S(2)}) collective-permute-start(bf16[2,32,1536]{2,1,0:T(8,128)(2,1)S(1)} %pad_maximum_fusion.2), channel_id=1, source_target_pairs={{0,1},{1,0},{2,3},{3,2},{4,5},{5,4},{6,7},{7,6},{8,9},{9,8},{10,11... | collective-permute-start | bytes 589832 | tf_op jit(solution)/shard_map/cond/branch_2_fun/ppermute | solution.py:28
  17.2 11.4 %collective-permute-start.30 = (bf16[2,128,768]{2,1,0:T(8,128)(2,1)S(1)}, bf16[2,128,768]{2,1,0:T(8,128)(2,1)S(1)}, u32[]{:S(2)}, u32[]{:S(2)}) collective-permute-start(bf16[2,128,768]{2,1,0:T(8,128)(2,1)S(1)} %constant_dynamic-update-slice_fusion.8.refs_6_), channel_id=1, source_target_pairs={{0,2},{1,3},{2,0},{3,1},{4,6},{5,7},{6,4},{7,5},{8,10},{9,11},{10,... | collective-permute-start | bytes 1179656 | tf_op jit(solution)/shard_map/cond/branch_2_fun/ppermute | solution.py:28
  18.5 2.6 %collective-permute-start.28 = (bf16[2,128,768]{2,1,0:T(8,128)(2,1)S(1)}, bf16[2,128,768]{2,1,0:T(8,128)(2,1)S(1)}, u32[]{:S(2)}, u32[]{:S(2)}) collective-permute-start(bf16[2,128,768]{2,1,0:T(8,128)(2,1)S(1)} %constant_dynamic-update-slice_fusion.8.refs_6_), channel_id=1, source_target_pairs={{0,1},{1,0},{2,3},{3,2},{4,5},{5,4},{6,7},{7,6},{8,9},{9,8},{10,11... | collective-permute-start | bytes 1179656 | tf_op jit(solution)/shard_map/cond/branch_2_fun/ppermute | solution.py:28
  26.3 2.5 %collective-permute-start.31 = (bf16[2,128,768]{2,1,0:T(8,128)(2,1)S(1)}, bf16[2,128,768]{2,1,0:T(8,128)(2,1)S(1)}, u32[]{:S(2)}, u32[]{:S(2)}) collective-permute-start(bf16[2,128,768]{2,1,0:T(8,128)(2,1)S(1)} %constant_dynamic-update-slice_fusion.10.refs_6_), channel_id=1, source_target_pairs={{0,1},{1,0},{2,3},{3,2},{4,5},{5,4},{6,7},{7,6},{8,9},{9,8},{10,11... | collective-permute-start | bytes 1179656 | tf_op jit(solution)/shard_map/cond/branch_2_fun/ppermute | solution.py:28
  27.4 10.7 %collective-permute-start.29 = (bf16[2,128,768]{2,1,0:T(8,128)(2,1)S(1)}, bf16[2,128,768]{2,1,0:T(8,128)(2,1)S(1)}, u32[]{:S(2)}, u32[]{:S(2)}) collective-permute-start(bf16[2,128,768]{2,1,0:T(8,128)(2,1)S(1)} %constant_dynamic-update-slice_fusion.10.refs_6_), channel_id=1, source_target_pairs={{0,2},{1,3},{2,0},{3,1},{4,6},{5,7},{6,4},{7,5},{8,10},{9,11},{10,... | collective-permute-start | bytes 1179656 | tf_op jit(solution)/shard_map/cond/branch_2_fun/ppermute | solution.py:28
  28.8 9.3 %collective-permute-start.32 = (bf16[2,128,768]{2,1,0:T(8,128)(2,1)S(1)}, bf16[2,128,768]{2,1,0:T(8,128)(2,1)S(1)}, u32[]{:S(2)}, u32[]{:S(2)}) collective-permute-start(bf16[2,128,768]{2,1,0:T(8,128)(2,1)S(1)} %collective-permute-done.30.refs_7_), channel_id=1, source_target_pairs={{0,1},{1,0},{2,3},{3,2},{4,5},{5,4},{6,7},{7,6},{8,9},{9,8},{10,11... | collective-permute-start | bytes 1179656 | tf_op jit(solution)/shard_map/cond/branch_2_fun/ppermute | solution.py:28
  38.1 3.7 %collective-permute-start.33 = (bf16[2,128,768]{2,1,0:T(8,128)(2,1)S(1)}, bf16[2,128,768]{2,1,0:T(8,128)(2,1)S(1)}, u32[]{:S(2)}, u32[]{:S(2)}) collective-permute-start(bf16[2,128,768]{2,1,0:T(8,128)(2,1)S(1)} %collective-permute-done.29.refs_5_), channel_id=1, source_target_pairs={{0,1},{1,0},{2,3},{3,2},{4,5},{5,4},{6,7},{7,6},{8,9},{9,8},{10,11... | collective-permute-start | bytes 1179656 | tf_op jit(solution)/shard_map/cond/branch_2_fun/ppermute | solution.py:28
  44.2 1.0 %copy-start.9 = (bf16[2,32,8192]{2,1,0:T(8,128)(2,1)}, bf16[2,32,8192]{2,1,0:T(8,128)(2,1)S(1)}, u32[]{:S(2)}) copy-start(bf16[2,32,8192]{2,1,0:T(8,128)(2,1)S(1)} %get-tuple-element.323) | copy-start | bytes 3145732

commit v3 on v2

--- a/solution.py
+++ b/solution.py
@@ -12,7 +12,7 @@
 LAGS = 64
 ROUNDS = 2
 LAG_STEP = 16
-LAST_LAG_STEP = 32
+LONG_LAG_STEP = 32
 BIN_STEP = 256
 PARTS = 2
 SWITCH_BLOCKS = 8
@@ -109,15 +109,15 @@
     return outs[0], outs[1:-1], outs[-1][0]
 
 
-def correlate_kernel(plan, shift, first, last, *refs):
+def correlate_kernel(plan, shift, first, scaling, last, *refs):
     refs = list(refs)
-    lag_step = LAST_LAG_STEP if last else LAG_STEP
+    lag_step = LONG_LAG_STEP if len(plan) < 3 else LAG_STEP
     take = lambda count: [refs.pop(0) for _ in range(count)]
     cos_ref, sin_ref = take(2)
-    if first:
+    if not first:
+        (total_ref,) = take(1)
+    if scaling:
         masks_ref, matching_ref = take(2)
-    else:
-        (total_ref,) = take(1)
     if last:
         scale_ref, matching_ref = take(2)
     own_refs = take(1 + max(piece[0] for piece in plan))
@@ -131,7 +131,7 @@
             lhs, rhs, (((1,), (1,)), ((), ())), preferred_element_type=jnp.float32
         )
 
-    if first:
+    if scaling:
         new_scale_ref, counts_ref = refs[1], refs[2]
         block_id, slot = lax.axis_index("chan"), lax.axis_index("win")
         own_at = pl.ds(pl.multiple_of(block_id * block, block), block)
@@ -209,7 +209,7 @@
             copy(index).wait()
 
 
-def correlate(state, masks, matching, shift, pieces, last):
+def correlate(state, masks, matching, shift, pieces, scaling, last):
     first = state is None
     own, plan = [], []
     for rows, first_bin, stack in pieces:
@@ -222,12 +222,12 @@
     cos, sin = tables(two_bins // 2)
     arrays = [jnp.asarray(cos), jnp.asarray(sin)]
     specs = [VMEM] * 2
-    if first:
+    if not first:
+        arrays.append(state[0])
+        specs.append(VMEM)
+    if scaling:
         arrays += [masks, matching]
         specs += [VMEM, SMEM]
-    else:
-        arrays.append(state[0])
-        specs.append(VMEM)
     if last:
         arrays += [state[1], matching]
         specs += [VMEM, SMEM]
@@ -240,16 +240,16 @@
         outs, out_specs = [final], [pl.BlockSpec(memory_space=pl.ANY)]
         scratch = [
             pltpu.VMEM(final.shape, final.dtype),
-            pltpu.SemaphoreType.DMA((LAGS // LAST_LAG_STEP,)),
+            pltpu.SemaphoreType.DMA((LAGS // LONG_LAG_STEP,)),
         ]
-    elif first:
+    elif scaling:
         outs, out_specs = [running, shape((ROUNDS, rows, block), jnp.float32)], [VMEM] * 2
         scratch = [pltpu.VMEM((block, block), jnp.float32)]
     else:
         outs, out_specs = [running], [VMEM]
     depth = 2 * sum(w_count * width for _, _, width in plan)
     result = pl.pallas_call(
-        functools.partial(correlate_kernel, plan, shift, first, last),
+        functools.partial(correlate_kernel, plan, shift, first, scaling, last),
         out_shape=outs,
         in_specs=specs + [VMEM] * len(others),
         out_specs=out_specs,
@@ -263,7 +263,7 @@
     )(*arrays, *others)
     if last:
         return result[0]
-    return (result[0], result[1] if first else state[1])
+    return [result[0], *(result[1:] if scaling else [] if first else state[1:])]
 
 
 def combine(masks, matching, shift, own, sides):
@@ -298,7 +298,7 @@
             early.add(steps[ahead])
             pieces.append((own[steps[ahead][0]], steps[ahead][1] * width, coming))
         pieces.append((own[d | low], n * width, across))
-        state = correlate(state, masks, matching, shift, pieces, ahead == len(steps))
+        state = correlate(state, masks, matching, shift, pieces, number == 1, ahead == len(steps))
     return state
 
 

time: 45.4 us -> 44.7 us (0.985)
  Pallas kernels: 14.2 us -> 13.5 us
    pallas_call x4, Pallas kernels: 12.7 us -> 12 us  [correlate(): pl.pallas_call(functools.partial(correlate_kernel, plan, shift, first, sc...]
  transfers between devices with their start and end apart: 12 -> 12, of which waited for: 5 -> 5; matrix products, arithmetic and copies ran while one was open for 0% -> 0% of each run, Pallas kernels for 23% -> 22%
where the time goes in v3:
time: 44.7 us; the launch traced here: 44.8 us
  starting transfers between devices  15.9 us (36%)
  Pallas kernels  13.5 us (30%)
  waiting for transfers between devices  12.1 us (27%)
  local copies, waits for them, and re-layouts  2.05 us (5%)
  between operations  0.68 us (2%)
  loops' own time  0.55 us (1%)
    ppermute x12, starting transfers between devices, flip(): lax.ppermute(value, axis, [(i, i ^ bits) for i in range(lax.axis_size(axi...  15.9 us
    ppermute x12, waiting for transfers between devices, flip(): lax.ppermute(value, axis, [(i, i ^ bits) for i in range(lax.axis_size(axi...  12.1 us
    pallas_call x4, Pallas kernels, correlate(): pl.pallas_call(functools.partial(correlate_kernel, plan, shift, first, sc...  12 us
    unnamed x4, local copies, waits for them, and re-layouts  1.96 us
    pallas_call x1, Pallas kernels, prepare(): pl.pallas_call(prepare_kernel, out_shape=[shape(spectra.shape, jnp.bfloat...  1.46 us
  transfers between devices with their start and end apart: 12, of which 5 were waited for; matrix products, arithmetic and copies ran while one was open for 0% of the time, Pallas kernels for 22%

profile of v3, /device:TPU:1, one launch (start us, length us, event | category | flops | bytes accessed | tf_op | source)
XLA Modules:
  0.0 44.8 jit_solution(8238316884779083655)
XLA Ops:
  0.0 1.0 %copy-done = bf16[1,128,1536]{2,1,0:T(8,128)(2,1)S(1)} copy-done((bf16[1,128,1536]{2,1,0:T(8,128)(2,1)S(1)}, bf16[1,128,1536]{2,1,0:T(8,128)(2,1)}, u32[]{:S(2)}) %copy-start) | copy-done | bytes 393240
  1.0 1.5 %shard_map.329 = (bf16[1,128,1536]{2,1,0:T(8,128)(2,1)S(1)}, bf16[1,128,768]{2,1,0:T(8,128)(2,1)S(1)}, bf16[1,128,768]{2,1,0:T(8,128)(2,1)S(1)}, s32[1]{0:T(128)}) custom-call(bf16[1,128,1536]{2,1,0:T(8,128)(2,1)S(1)} %copy-done, s32[4,1024]{1,0:T(4,128)} %masks_ref.1, s32[2,8]{1,0:T(2,128)} %matching_ref.1), custom_call_target="tpu_custom_call" | custom-call | tf_op jit(solution)/shard_map/pallas_call | solution.py:102
  3.1 40.7 %conditional.1 = (bf16[2,32,8192]{2,1,0:T(8,128)(2,1)S(1)}) conditional(s32[]{:T(128)} %bitcast, (bf16[1,128,1536]{2,1,0:T(8,128)(2,1)S(1)}, bf16[1,128,768]{2,1,0:T(8,128)(2,1)S(1)}, bf16[1,128,768]{2,1,0:T(8,128)(2,1)S(1)}, f32[64,768]{1,0:T(8,128)}, f32[64,768]{1,0:T(8,128)}, /*index=5*/f32[64,768]{1,0:T(8,128)}, ...), branch_computations={%region_0.1_spmd, %region_1.2_spmd, %region_2.3_spmd, %region_3.4_... | conditional | flops 6442942464 | bytes 23266200 | solution.py:329
  3.3 0.0 copy-start.3
  3.3 0.0 copy-start.7
  3.3 4.2 %collective-permute-start.27 = (bf16[1,128,768]{2,1,0:T(8,128)(2,1)S(1)}, bf16[1,128,768]{2,1,0:T(8,128)(2,1)S(1)}, u32[]{:S(2)}, u32[]{:S(2)}) collective-permute-start(bf16[1,128,768]{2,1,0:T(8,128)(2,1)S(1)} %get-tuple-element.178), channel_id=1, source_target_pairs={{0,20},{4,16},{8,28},{12,24},{16,4},{20,0},{24,12},{28,8},{1,21},{... | collective-permute-start | bytes 589832 | tf_op jit(solution)/shard_map/cond/branch_2_fun/ppermute | solution.py:28
  7.5 1.3 %collective-permute-start.26 = (bf16[1,128,768]{2,1,0:T(8,128)(2,1)S(1)}, bf16[1,128,768]{2,1,0:T(8,128)(2,1)S(1)}, u32[]{:S(2)}, u32[]{:S(2)}) collective-permute-start(bf16[1,128,768]{2,1,0:T(8,128)(2,1)S(1)} %get-tuple-element.178), channel_id=1, source_target_pairs={{0,8},{4,12},{8,0},{12,4},{16,24},{20,28},{24,16},{28,20},{1,9},{5... | collective-permute-start | bytes 589832 | tf_op jit(solution)/shard_map/cond/branch_2_fun/ppermute | solution.py:28
  8.8 1.3 %collective-permute-start.22 = (bf16[1,64,1536]{2,1,0:T(8,128)(2,1)S(1)}, bf16[1,64,1536]{2,1,0:T(8,128)(2,1)S(1)}, u32[]{:S(2)}, u32[]{:S(2)}) collective-permute-start(bf16[1,64,1536]{2,1,0:T(8,128)(2,1)S(1)} %get-tuple-element.248), channel_id=1, source_target_pairs={{0,2},{1,3},{2,0},{3,1},{4,6},{5,7},{6,4},{7,5},{8,10},{9,11},{10,... | collective-permute-start | bytes 589832 | tf_op jit(solution)/shard_map/cond/branch_2_fun/ppermute | solution.py:28
  10.1 3.9 %collective-permute-done.22 = bf16[1,64,1536]{2,1,0:T(8,128)(2,1)S(1)} collective-permute-done((bf16[1,64,1536]{2,1,0:T(8,128)(2,1)S(1)}, bf16[1,64,1536]{2,1,0:T(8,128)(2,1)S(1)}, u32[]{:S(2)}, u32[]{:S(2)}) %collective-permute-start.22) | collective-permute-done | bytes 196640 | tf_op jit(solution)/shard_map/cond/branch_2_fun/ppermute | solution.py:28
  14.1 0.2 collective-permute-start.24
  14.2 0.4 collective-permute-start.23
  14.7 2.5 %collective-permute-start.25 = (bf16[2,32,1536]{2,1,0:T(8,128)(2,1)S(1)}, bf16[2,32,1536]{2,1,0:T(8,128)(2,1)S(1)}, u32[]{:S(2)}, u32[]{:S(2)}) collective-permute-start(bf16[2,32,1536]{2,1,0:T(8,128)(2,1)S(1)} %pad_maximum_fusion.2), channel_id=1, source_target_pairs={{0,1},{1,0},{2,3},{3,2},{4,5},{5,4},{6,7},{7,6},{8,9},{9,8},{10,11... | collective-permute-start | bytes 589832 | tf_op jit(solution)/shard_map/cond/branch_2_fun/ppermute | solution.py:28
  17.1 0.0 collective-permute-done.26
  17.2 1.3 %collective-permute-start.30 = (bf16[2,128,768]{2,1,0:T(8,128)(2,1)S(1)}, bf16[2,128,768]{2,1,0:T(8,128)(2,1)S(1)}, u32[]{:S(2)}, u32[]{:S(2)}) collective-permute-start(bf16[2,128,768]{2,1,0:T(8,128)(2,1)S(1)} %constant_dynamic-update-slice_fusion.8.refs_4_), channel_id=1, source_target_pairs={{0,2},{1,3},{2,0},{3,1},{4,6},{5,7},{6,4},{7,5},{8,10},{9,11},{10,... | collective-permute-start | bytes 1179656 | tf_op jit(solution)/shard_map/cond/branch_2_fun/ppermute | solution.py:28
  18.5 1.2 %collective-permute-start.28 = (bf16[2,128,768]{2,1,0:T(8,128)(2,1)S(1)}, bf16[2,128,768]{2,1,0:T(8,128)(2,1)S(1)}, u32[]{:S(2)}, u32[]{:S(2)}) collective-permute-start(bf16[2,128,768]{2,1,0:T(8,128)(2,1)S(1)} %constant_dynamic-update-slice_fusion.8.refs_4_), channel_id=1, source_target_pairs={{0,1},{1,0},{2,3},{3,2},{4,5},{5,4},{6,7},{7,6},{8,9},{9,8},{10,11... | collective-permute-start | bytes 1179656 | tf_op jit(solution)/shard_map/cond/branch_2_fun/ppermute | solution.py:28
  19.7 0.0 collective-permute-done.25
  19.7 1.3 %collective-permute-done.28.refs_5_ = bf16[2,128,768]{2,1,0:T(8,128)(2,1)S(1)} collective-permute-done((bf16[2,128,768]{2,1,0:T(8,128)(2,1)S(1)}, bf16[2,128,768]{2,1,0:T(8,128)(2,1)S(1)}, u32[]{:S(2)}, u32[]{:S(2)}) %collective-permute-start.28) | collective-permute-done | bytes 393248 | tf_op jit(solution)/shard_map/cond/branch_2_fun/ppermute | solution.py:28
  21.1 2.5 %branch_2_fun.4.refs_2_ = f32[2048,256]{1,0:T(8,128)S(1)} custom-call(f32[64,768]{1,0:T(8,128)S(1)} %copy-done.7, f32[64,768]{1,0:T(8,128)S(1)} %copy-done.3, bf16[1,32,1536]{2,1,0:T(8,128)(2,1)S(1)} %get-tuple-element.254.refs_2_.refs_5_, bf16[1,32,1536]{2,1,0:T(8,128)(2,1)S(1)} %get-tuple-element.250.refs_3_.refs_7_, ...), custom_call_target="tpu_custom_call" | custom-call | flops 1610612736 | bytes 884736 | tf_op jit(solution)/shard_map/cond/branch_2_fun/pallas_call | solution.py:251
  23.6 2.6 %collective-permute-done.24 = bf16[1,128,768]{2,1,0:T(8,128)(2,1)S(1)} collective-permute-done((bf16[1,128,768]{2,1,0:T(8,128)(2,1)S(1)}, bf16[1,128,768]{2,1,0:T(8,128)(2,1)S(1)}, u32[]{:S(2)}, u32[]{:S(2)}) %collective-permute-start.24) | collective-permute-done | bytes 196640 | tf_op jit(solution)/shard_map/cond/branch_2_fun/ppermute | solution.py:28
  26.2 0.0 collective-permute-done.23
  26.2 1.1 %collective-permute-start.31 = (bf16[2,128,768]{2,1,0:T(8,128)(2,1)S(1)}, bf16[2,128,768]{2,1,0:T(8,128)(2,1)S(1)}, u32[]{:S(2)}, u32[]{:S(2)}) collective-permute-start(bf16[2,128,768]{2,1,0:T(8,128)(2,1)S(1)} %constant_dynamic-update-slice_fusion.10.refs_8_), channel_id=1, source_target_pairs={{0,1},{1,0},{2,3},{3,2},{4,5},{5,4},{6,7},{7,6},{8,9},{9,8},{10,11... | collective-permute-start | bytes 1179656 | tf_op jit(solution)/shard_map/cond/branch_2_fun/ppermute | solution.py:28
  27.4 1.2 %collective-permute-start.29 = (bf16[2,128,768]{2,1,0:T(8,128)(2,1)S(1)}, bf16[2,128,768]{2,1,0:T(8,128)(2,1)S(1)}, u32[]{:S(2)}, u32[]{:S(2)}) collective-permute-start(bf16[2,128,768]{2,1,0:T(8,128)(2,1)S(1)} %constant_dynamic-update-slice_fusion.10.refs_8_), channel_id=1, source_target_pairs={{0,2},{1,3},{2,0},{3,1},{4,6},{5,7},{6,4},{7,5},{8,10},{9,11},{10,... | collective-permute-start | bytes 1179656 | tf_op jit(solution)/shard_map/cond/branch_2_fun/ppermute | solution.py:28
  28.6 0.0 collective-permute-done.30.refs_9_
  28.6 0.1 collective-permute-done.31.refs_10_
  28.7 0.4 collective-permute-start.32
  29.1 4.8 %branch_2_fun.5 = (f32[2048,256]{1,0:T(8,128)S(1)}, f32[2,32,128]{2,1,0:T(8,128)S(1)}) custom-call(f32[64,768]{1,0:T(8,128)S(1)} %copy-done.7, f32[64,768]{1,0:T(8,128)S(1)} %copy-done.3, f32[2048,256]{1,0:T(8,128)S(1)} %branch_2_fun.4.refs_2_, s32[4,1024]{1,0:T(4,128)S(1)} %copy-done.16, s32[2,8]{1,0:T(2,128)S(1)} %copy-done.12, ...), custom_call_target="tpu_custom_call" | custom-call | flops 2415919104 | bytes 1327104 | tf_op jit(solution)/shard_map/cond/branch_2_fun/pallas_call | solution.py:251
  33.9 4.2 %collective-permute-done.29.refs_5_ = bf16[2,128,768]{2,1,0:T(8,128)(2,1)S(1)} collective-permute-done((bf16[2,128,768]{2,1,0:T(8,128)(2,1)S(1)}, bf16[2,128,768]{2,1,0:T(8,128)(2,1)S(1)}, u32[]{:S(2)}, u32[]{:S(2)}) %collective-permute-start.29) | collective-permute-done | bytes 393248 | tf_op jit(solution)/shard_map/cond/branch_2_fun/ppermute | solution.py:28
  38.1 0.9 %collective-permute-start.33 = (bf16[2,128,768]{2,1,0:T(8,128)(2,1)S(1)}, bf16[2,128,768]{2,1,0:T(8,128)(2,1)S(1)}, u32[]{:S(2)}, u32[]{:S(2)}) collective-permute-start(bf16[2,128,768]{2,1,0:T(8,128)(2,1)S(1)} %collective-permute-done.29.refs_5_), channel_id=1, source_target_pairs={{0,1},{1,0},{2,3},{3,2},{4,5},{5,4},{6,7},{7,6},{8,9},{9,8},{10,11... | collective-permute-start | bytes 1179656 | tf_op jit(solution)/shard_map/cond/branch_2_fun/ppermute | solution.py:28
  38.9 2.5 %branch_2_fun.6.refs_2_ = f32[2048,256]{1,0:T(8,128)S(1)} custom-call(f32[64,768]{1,0:T(8,128)S(1)} %copy-done.7, f32[64,768]{1,0:T(8,128)S(1)} %copy-done.3, f32[2048,256]{1,0:T(8,128)S(1)} %get-tuple-element.191.refs_2_, bf16[1,32,1536]{2,1,0:T(8,128)(2,1)S(1)} %get-tuple-element.251.refs_6_.refs_3_, ...), custom_call_target="tpu_custom_call" | custom-call | flops 1610612736 | bytes 884736 | tf_op jit(solution)/shard_map/cond/branch_2_fun/pallas_call | solution.py:251
  41.5 2.2 %branch_2_fun.7 = bf16[2,32,8192]{2,1,0:T(8,128)(2,1)S(1)} custom-call(f32[64,768]{1,0:T(8,128)S(1)} %copy-done.7, f32[64,768]{1,0:T(8,128)S(1)} %copy-done.3, f32[2048,256]{1,0:T(8,128)S(1)} %branch_2_fun.6.refs_2_, f32[2,32,128]{2,1,0:T(8,128)S(1)} %get-tuple-element.194.refs_3_, s32[2,8]{1,0:T(2,128)S(1)} %copy-done.12, ...), custom_call_target="tpu_custom_call" | custom-call | flops 805306368 | bytes 442368 | tf_op jit(solution)/shard_map/cond/branch_2_fun/pallas_call | solution.py:251
  43.9 0.0 copy-start.9
  43.9 1.0 %copy-done.9 = bf16[2,32,8192]{2,1,0:T(8,128)(2,1)} copy-done((bf16[2,32,8192]{2,1,0:T(8,128)(2,1)}, bf16[2,32,8192]{2,1,0:T(8,128)(2,1)S(1)}, u32[]{:S(2)}) %copy-start.9) | copy-done | bytes 1048600
  (19 shorter events, 0.2 us)
Async XLA Ops:
  0.0 1.0 %copy-start = (bf16[1,128,1536]{2,1,0:T(8,128)(2,1)S(1)}, bf16[1,128,1536]{2,1,0:T(8,128)(2,1)}, u32[]{:S(2)}) copy-start(bf16[1,128,1536]{2,1,0:T(8,128)(2,1)} %spectra_ref.1) | copy-start | bytes 1179652
  3.3 17.7 %copy-start.3 = (f32[64,768]{1,0:T(8,128)S(1)}, f32[64,768]{1,0:T(8,128)}, u32[]{:S(2)}) copy-start(f32[64,768]{1,0:T(8,128)} %get-tuple-element.169.refs_1_) | copy-start | bytes 589828 | tf_op jit(solution)/shard_map/cond
  3.3 17.7 %copy-start.7 = (f32[64,768]{1,0:T(8,128)S(1)}, f32[64,768]{1,0:T(8,128)}, u32[]{:S(2)}) copy-start(f32[64,768]{1,0:T(8,128)} %get-tuple-element.168.refs_0_) | copy-start | bytes 589828 | tf_op jit(solution)/shard_map/cond
  3.3 13.8 %collective-permute-start.27 = (bf16[1,128,768]{2,1,0:T(8,128)(2,1)S(1)}, bf16[1,128,768]{2,1,0:T(8,128)(2,1)S(1)}, u32[]{:S(2)}, u32[]{:S(2)}) collective-permute-start(bf16[1,128,768]{2,1,0:T(8,128)(2,1)S(1)} %get-tuple-element.178), channel_id=1, source_target_pairs={{0,20},{4,16},{8,28},{12,24},{16,4},{20,0},{24,12},{28,8},{1,21},{... | collective-permute-start | bytes 589832 | tf_op jit(solution)/shard_map/cond/branch_2_fun/ppermute | solution.py:28
  7.5 9.6 %collective-permute-start.26 = (bf16[1,128,768]{2,1,0:T(8,128)(2,1)S(1)}, bf16[1,128,768]{2,1,0:T(8,128)(2,1)S(1)}, u32[]{:S(2)}, u32[]{:S(2)}) collective-permute-start(bf16[1,128,768]{2,1,0:T(8,128)(2,1)S(1)} %get-tuple-element.178), channel_id=1, source_target_pairs={{0,8},{4,12},{8,0},{12,4},{16,24},{20,28},{24,16},{28,20},{1,9},{5... | collective-permute-start | bytes 589832 | tf_op jit(solution)/shard_map/cond/branch_2_fun/ppermute | solution.py:28
  8.8 5.2 %collective-permute-start.22 = (bf16[1,64,1536]{2,1,0:T(8,128)(2,1)S(1)}, bf16[1,64,1536]{2,1,0:T(8,128)(2,1)S(1)}, u32[]{:S(2)}, u32[]{:S(2)}) collective-permute-start(bf16[1,64,1536]{2,1,0:T(8,128)(2,1)S(1)} %get-tuple-element.248), channel_id=1, source_target_pairs={{0,2},{1,3},{2,0},{3,1},{4,6},{5,7},{6,4},{7,5},{8,10},{9,11},{10,... | collective-permute-start | bytes 589832 | tf_op jit(solution)/shard_map/cond/branch_2_fun/ppermute | solution.py:28
  14.1 12.1 %collective-permute-start.24 = (bf16[1,128,768]{2,1,0:T(8,128)(2,1)S(1)}, bf16[1,128,768]{2,1,0:T(8,128)(2,1)S(1)}, u32[]{:S(2)}, u32[]{:S(2)}) collective-permute-start(bf16[1,128,768]{2,1,0:T(8,128)(2,1)S(1)} %get-tuple-element.174), channel_id=1, source_target_pairs={{0,20},{4,16},{8,28},{12,24},{16,4},{20,0},{24,12},{28,8},{1,21},{... | collective-permute-start | bytes 589832 | tf_op jit(solution)/shard_map/cond/branch_2_fun/ppermute | solution.py:28
  14.2 12.0 %collective-permute-start.23 = (bf16[1,128,768]{2,1,0:T(8,128)(2,1)S(1)}, bf16[1,128,768]{2,1,0:T(8,128)(2,1)S(1)}, u32[]{:S(2)}, u32[]{:S(2)}) collective-permute-start(bf16[1,128,768]{2,1,0:T(8,128)(2,1)S(1)} %get-tuple-element.174), channel_id=1, source_target_pairs={{0,8},{4,12},{8,0},{12,4},{16,24},{20,28},{24,16},{28,20},{1,9},{5... | collective-permute-start | bytes 589832 | tf_op jit(solution)/shard_map/cond/branch_2_fun/ppermute | solution.py:28
  14.7 5.1 %collective-permute-start.25 = (bf16[2,32,1536]{2,1,0:T(8,128)(2,1)S(1)}, bf16[2,32,1536]{2,1,0:T(8,128)(2,1)S(1)}, u32[]{:S(2)}, u32[]{:S(2)}) collective-permute-start(bf16[2,32,1536]{2,1,0:T(8,128)(2,1)S(1)} %pad_maximum_fusion.2), channel_id=1, source_target_pairs={{0,1},{1,0},{2,3},{3,2},{4,5},{5,4},{6,7},{7,6},{8,9},{9,8},{10,11... | collective-permute-start | bytes 589832 | tf_op jit(solution)/shard_map/cond/branch_2_fun/ppermute | solution.py:28
  17.2 11.4 %collective-permute-start.30 = (bf16[2,128,768]{2,1,0:T(8,128)(2,1)S(1)}, bf16[2,128,768]{2,1,0:T(8,128)(2,1)S(1)}, u32[]{:S(2)}, u32[]{:S(2)}) collective-permute-start(bf16[2,128,768]{2,1,0:T(8,128)(2,1)S(1)} %constant_dynamic-update-slice_fusion.8.refs_4_), channel_id=1, source_target_pairs={{0,2},{1,3},{2,0},{3,1},{4,6},{5,7},{6,4},{7,5},{8,10},{9,11},{10,... | collective-permute-start | bytes 1179656 | tf_op jit(solution)/shard_map/cond/branch_2_fun/ppermute | solution.py:28
  18.5 2.6 %collective-permute-start.28 = (bf16[2,128,768]{2,1,0:T(8,128)(2,1)S(1)}, bf16[2,128,768]{2,1,0:T(8,128)(2,1)S(1)}, u32[]{:S(2)}, u32[]{:S(2)}) collective-permute-start(bf16[2,128,768]{2,1,0:T(8,128)(2,1)S(1)} %constant_dynamic-update-slice_fusion.8.refs_4_), channel_id=1, source_target_pairs={{0,1},{1,0},{2,3},{3,2},{4,5},{5,4},{6,7},{7,6},{8,9},{9,8},{10,11... | collective-permute-start | bytes 1179656 | tf_op jit(solution)/shard_map/cond/branch_2_fun/ppermute | solution.py:28
  21.1 8.0 %copy-start.12 = (s32[2,8]{1,0:T(2,128)S(1)}, s32[2,8]{1,0:T(2,128)}, u32[]{:S(2)}) copy-start(s32[2,8]{1,0:T(2,128)} %get-tuple-element.187.refs_4_) | copy-start | bytes 196 | tf_op jit(solution)/shard_map/cond
  21.1 8.0 %copy-start.16 = (s32[4,1024]{1,0:T(4,128)S(1)}, s32[4,1024]{1,0:T(4,128)}, u32[]{:S(2)}) copy-start(s32[4,1024]{1,0:T(4,128)} %get-tuple-element.186.refs_3_) | copy-start | bytes 49156 | tf_op jit(solution)/shard_map/cond
  26.2 2.5 %collective-permute-start.31 = (bf16[2,128,768]{2,1,0:T(8,128)(2,1)S(1)}, bf16[2,128,768]{2,1,0:T(8,128)(2,1)S(1)}, u32[]{:S(2)}, u32[]{:S(2)}) collective-permute-start(bf16[2,128,768]{2,1,0:T(8,128)(2,1)S(1)} %constant_dynamic-update-slice_fusion.10.refs_8_), channel_id=1, source_target_pairs={{0,1},{1,0},{2,3},{3,2},{4,5},{5,4},{6,7},{7,6},{8,9},{9,8},{10,11... | collective-permute-start | bytes 1179656 | tf_op jit(solution)/shard_map/cond/branch_2_fun/ppermute | solution.py:28
  27.4 10.7 %collective-permute-start.29 = (bf16[2,128,768]{2,1,0:T(8,128)(2,1)S(1)}, bf16[2,128,768]{2,1,0:T(8,128)(2,1)S(1)}, u32[]{:S(2)}, u32[]{:S(2)}) collective-permute-start(bf16[2,128,768]{2,1,0:T(8,128)(2,1)S(1)} %constant_dynamic-update-slice_fusion.10.refs_8_), channel_id=1, source_target_pairs={{0,2},{1,3},{2,0},{3,1},{4,6},{5,7},{6,4},{7,5},{8,10},{9,11},{10,... | collective-permute-start | bytes 1179656 | tf_op jit(solution)/shard_map/cond/branch_2_fun/ppermute | solution.py:28
  28.7 9.3 %collective-permute-start.32 = (bf16[2,128,768]{2,1,0:T(8,128)(2,1)S(1)}, bf16[2,128,768]{2,1,0:T(8,128)(2,1)S(1)}, u32[]{:S(2)}, u32[]{:S(2)}) collective-permute-start(bf16[2,128,768]{2,1,0:T(8,128)(2,1)S(1)} %collective-permute-done.30.refs_9_), channel_id=1, source_target_pairs={{0,1},{1,0},{2,3},{3,2},{4,5},{5,4},{6,7},{7,6},{8,9},{9,8},{10,11... | collective-permute-start | bytes 1179656 | tf_op jit(solution)/shard_map/cond/branch_2_fun/ppermute | solution.py:28
  38.1 3.4 %collective-permute-start.33 = (bf16[2,128,768]{2,1,0:T(8,128)(2,1)S(1)}, bf16[2,128,768]{2,1,0:T(8,128)(2,1)S(1)}, u32[]{:S(2)}, u32[]{:S(2)}) collective-permute-start(bf16[2,128,768]{2,1,0:T(8,128)(2,1)S(1)} %collective-permute-done.29.refs_5_), channel_id=1, source_target_pairs={{0,1},{1,0},{2,3},{3,2},{4,5},{5,4},{6,7},{7,6},{8,9},{9,8},{10,11... | collective-permute-start | bytes 1179656 | tf_op jit(solution)/shard_map/cond/branch_2_fun/ppermute | solution.py:28
  43.9 1.0 %copy-start.9 = (bf16[2,32,8192]{2,1,0:T(8,128)(2,1)}, bf16[2,32,8192]{2,1,0:T(8,128)(2,1)S(1)}, u32[]{:S(2)}) copy-start(bf16[2,32,8192]{2,1,0:T(8,128)(2,1)S(1)} %get-tuple-element.315) | copy-start | bytes 3145732

commit v4 on v3

--- a/solution.py
+++ b/solution.py
@@ -285,11 +285,13 @@
                 held[d, n] = flip(before, "win", bit)
         return held[d, n], state
 
-    early = set()
+    early, waiting = set(), []
     for number, (d, n) in enumerate(steps):
         here, state = stack(d, n, state)
         across = flip(here, "win", low)
-        pieces = [] if (d, n) in early else [(own[d], n * width, here)]
+        if number == 0:
+            here, own = after(here, own)
+        pieces = waiting + ([] if (d, n) in early else [(own[d], n * width, here)])
         ahead = number + 1
         if 0 < number and ahead < len(steps) and steps[ahead][0] != 0:
             coming, state = stack(*steps[ahead], state)
@@ -297,7 +299,9 @@
             held[steps[ahead]] = coming
             early.add(steps[ahead])
             pieces.append((own[steps[ahead][0]], steps[ahead][1] * width, coming))
-        pieces.append((own[d | low], n * width, across))
+        waiting = [(own[d | low], n * width, across)]
+        if number > 0 or ahead == len(steps):
+            pieces, waiting = pieces + waiting, []
         state = correlate(state, masks, matching, shift, pieces, number == 1, ahead == len(steps))
     return state
 

time: 44.7 us -> 45.2 us (1.011)
  starting transfers between devices: 15.9 us -> 15.4 us
  waiting for transfers between devices: 12.1 us -> 12.6 us
    ppermute x12, waiting for transfers between devices: 12.1 us -> 12.6 us  [flip(): lax.ppermute(value, axis, [(i, i ^ bits) for i in range(lax.axis_size(axi...]
    ppermute x12, starting transfers between devices: 15.9 us -> 15.4 us  [flip(): lax.ppermute(value, axis, [(i, i ^ bits) for i in range(lax.axis_size(axi...]
  transfers between devices with their start and end apart: 12 -> 12, of which waited for: 5 -> 4; matrix products, arithmetic and copies ran while one was open for 0% -> 0% of each run, Pallas kernels for 22% -> 22%
where the time goes in v4:
time: 45.2 us; the launch traced here: 44.9 us
  starting transfers between devices  15.4 us (34%)
  Pallas kernels  13.5 us (30%)
  waiting for transfers between devices  12.6 us (28%)
  local copies, waits for them, and re-layouts  2.06 us (5%)
  between operations  0.68 us (2%)
  loops' own time  0.58 us (1%)
    ppermute x12, starting transfers between devices, flip(): lax.ppermute(value, axis, [(i, i ^ bits) for i in range(lax.axis_size(axi...  15.4 us
    ppermute x12, waiting for transfers between devices, flip(): lax.ppermute(value, axis, [(i, i ^ bits) for i in range(lax.axis_size(axi...  12.6 us
    pallas_call x4, Pallas kernels, correlate(): pl.pallas_call(functools.partial(correlate_kernel, plan, shift, first, sc...  12 us
    unnamed x4, local copies, waits for them, and re-layouts  1.96 us
    pallas_call x1, Pallas kernels, prepare(): pl.pallas_call(prepare_kernel, out_shape=[shape(spectra.shape, jnp.bfloat...  1.46 us
  transfers between devices with their start and end apart: 12, of which 4 were waited for; matrix products, arithmetic and copies ran while one was open for 0% of the time, Pallas kernels for 22%

profile of v4, /device:TPU:1, one launch (start us, length us, event | category | flops | bytes accessed | tf_op | source)
XLA Modules:
  0.0 44.9 jit_solution(17228151563151590658)
XLA Ops:
  0.0 1.0 %copy-done = bf16[1,128,1536]{2,1,0:T(8,128)(2,1)S(1)} copy-done((bf16[1,128,1536]{2,1,0:T(8,128)(2,1)S(1)}, bf16[1,128,1536]{2,1,0:T(8,128)(2,1)}, u32[]{:S(2)}) %copy-start) | copy-done | bytes 393240
  1.0 1.5 %shard_map.329 = (bf16[1,128,1536]{2,1,0:T(8,128)(2,1)S(1)}, bf16[1,128,768]{2,1,0:T(8,128)(2,1)S(1)}, bf16[1,128,768]{2,1,0:T(8,128)(2,1)S(1)}, s32[1]{0:T(128)}) custom-call(bf16[1,128,1536]{2,1,0:T(8,128)(2,1)S(1)} %copy-done, s32[4,1024]{1,0:T(4,128)} %masks_ref.1, s32[2,8]{1,0:T(2,128)} %matching_ref.1), custom_call_target="tpu_custom_call" | custom-call | tf_op jit(solution)/shard_map/pallas_call | solution.py:102
  3.1 40.8 %conditional.1 = (bf16[2,32,8192]{2,1,0:T(8,128)(2,1)S(1)}) conditional(s32[]{:T(128)} %bitcast, (bf16[1,128,1536]{2,1,0:T(8,128)(2,1)S(1)}, bf16[1,128,768]{2,1,0:T(8,128)(2,1)S(1)}, bf16[1,128,768]{2,1,0:T(8,128)(2,1)S(1)}, f32[64,768]{1,0:T(8,128)}, f32[64,768]{1,0:T(8,128)}, /*index=5*/f32[64,768]{1,0:T(8,128)}, ...), branch_computations={%region_0.1_spmd, %region_1.2_spmd, %region_2.3_spmd, %region_3.4_... | conditional | flops 6442942464 | bytes 23266200 | solution.py:333
  3.3 0.0 copy-start.3
  3.3 0.0 copy-start.7
  3.3 4.2 %collective-permute-start.26 = (bf16[1,128,768]{2,1,0:T(8,128)(2,1)S(1)}, bf16[1,128,768]{2,1,0:T(8,128)(2,1)S(1)}, u32[]{:S(2)}, u32[]{:S(2)}) collective-permute-start(bf16[1,128,768]{2,1,0:T(8,128)(2,1)S(1)} %get-tuple-element.187), channel_id=1, source_target_pairs={{0,20},{4,16},{8,28},{12,24},{16,4},{20,0},{24,12},{28,8},{1,21},{... | collective-permute-start | bytes 589832 | tf_op jit(solution)/shard_map/cond/branch_2_fun/ppermute | solution.py:28
  7.5 1.3 %collective-permute-start.25 = (bf16[1,128,768]{2,1,0:T(8,128)(2,1)S(1)}, bf16[1,128,768]{2,1,0:T(8,128)(2,1)S(1)}, u32[]{:S(2)}, u32[]{:S(2)}) collective-permute-start(bf16[1,128,768]{2,1,0:T(8,128)(2,1)S(1)} %get-tuple-element.187), channel_id=1, source_target_pairs={{0,8},{4,12},{8,0},{12,4},{16,24},{20,28},{24,16},{28,20},{1,9},{5... | collective-permute-start | bytes 589832 | tf_op jit(solution)/shard_map/cond/branch_2_fun/ppermute | solution.py:28
  8.8 1.3 %collective-permute-start.22 = (bf16[1,64,1536]{2,1,0:T(8,128)(2,1)S(1)}, bf16[1,64,1536]{2,1,0:T(8,128)(2,1)S(1)}, u32[]{:S(2)}, u32[]{:S(2)}) collective-permute-start(bf16[1,64,1536]{2,1,0:T(8,128)(2,1)S(1)} %get-tuple-element.268), channel_id=1, source_target_pairs={{0,2},{1,3},{2,0},{3,1},{4,6},{5,7},{6,4},{7,5},{8,10},{9,11},{10,... | collective-permute-start | bytes 589832 | tf_op jit(solution)/shard_map/cond/branch_2_fun/ppermute | solution.py:28
  10.1 3.9 %collective-permute-done.22 = bf16[1,64,1536]{2,1,0:T(8,128)(2,1)S(1)} collective-permute-done((bf16[1,64,1536]{2,1,0:T(8,128)(2,1)S(1)}, bf16[1,64,1536]{2,1,0:T(8,128)(2,1)S(1)}, u32[]{:S(2)}, u32[]{:S(2)}) %collective-permute-start.22) | collective-permute-done | bytes 196640 | tf_op jit(solution)/shard_map/cond/branch_2_fun/ppermute | solution.py:28
  14.1 0.2 collective-permute-start.24
  14.2 0.4 collective-permute-start.23
  14.7 2.5 %collective-permute-start.27 = (bf16[2,32,1536]{2,1,0:T(8,128)(2,1)S(1)}, bf16[2,32,1536]{2,1,0:T(8,128)(2,1)S(1)}, u32[]{:S(2)}, u32[]{:S(2)}) collective-permute-start(bf16[2,32,1536]{2,1,0:T(8,128)(2,1)S(1)} %pad_maximum_fusion.2), channel_id=1, source_target_pairs={{0,1},{1,0},{2,3},{3,2},{4,5},{5,4},{6,7},{7,6},{8,9},{9,8},{10,11... | collective-permute-start | bytes 589832 | tf_op jit(solution)/shard_map/cond/branch_2_fun/ppermute | solution.py:28
  17.2 0.0 copy-start.12
  17.2 0.0 copy-start.16
  17.2 1.3 %collective-permute-start.29 = (bf16[2,128,768]{2,1,0:T(8,128)(2,1)S(1)}, bf16[2,128,768]{2,1,0:T(8,128)(2,1)S(1)}, u32[]{:S(2)}, u32[]{:S(2)}) collective-permute-start(bf16[2,128,768]{2,1,0:T(8,128)(2,1)S(1)} %constant_dynamic-update-slice_fusion.8.refs_3_), channel_id=1, source_target_pairs={{0,2},{1,3},{2,0},{3,1},{4,6},{5,7},{6,4},{7,5},{8,10},{9,11},{10,... | collective-permute-start | bytes 1179656 | tf_op jit(solution)/shard_map/cond/branch_2_fun/ppermute | solution.py:28
  18.5 0.0 collective-permute-done.27
  18.5 1.5 %branch_2_fun.4.refs_2_ = f32[2048,256]{1,0:T(8,128)S(1)} custom-call(f32[64,768]{1,0:T(8,128)S(1)} %copy-done.7, f32[64,768]{1,0:T(8,128)S(1)} %copy-done.3, bf16[1,32,1536]{2,1,0:T(8,128)(2,1)S(1)} %get-tuple-element.189.refs_2_.refs_6_, bf16[2,128,768]{2,1,0:T(8,128)(2,1)S(1)} %constant_dynamic-update-slice_fusion.8.refs_3_), custom_call_target="tpu_custom_call" | custom-call | flops 805306368 | bytes 442368 | tf_op jit(solution)/shard_map/cond/branch_2_fun/pallas_call | solution.py:251
  20.0 6.2 %collective-permute-done.24 = bf16[1,128,768]{2,1,0:T(8,128)(2,1)S(1)} collective-permute-done((bf16[1,128,768]{2,1,0:T(8,128)(2,1)S(1)}, bf16[1,128,768]{2,1,0:T(8,128)(2,1)S(1)}, u32[]{:S(2)}, u32[]{:S(2)}) %collective-permute-start.24) | collective-permute-done | bytes 196640 | tf_op jit(solution)/shard_map/cond/branch_2_fun/ppermute | solution.py:28
  26.2 1.1 %collective-permute-start.30 = (bf16[2,128,768]{2,1,0:T(8,128)(2,1)S(1)}, bf16[2,128,768]{2,1,0:T(8,128)(2,1)S(1)}, u32[]{:S(2)}, u32[]{:S(2)}) collective-permute-start(bf16[2,128,768]{2,1,0:T(8,128)(2,1)S(1)} %constant_dynamic-update-slice_fusion.10.refs_9_), channel_id=1, source_target_pairs={{0,1},{1,0},{2,3},{3,2},{4,5},{5,4},{6,7},{7,6},{8,9},{9,8},{10,11... | collective-permute-start | bytes 1179656 | tf_op jit(solution)/shard_map/cond/branch_2_fun/ppermute | solution.py:28
  27.4 0.1 collective-permute-start.32
  27.5 1.2 %collective-permute-start.28 = (bf16[2,128,768]{2,1,0:T(8,128)(2,1)S(1)}, bf16[2,128,768]{2,1,0:T(8,128)(2,1)S(1)}, u32[]{:S(2)}, u32[]{:S(2)}) collective-permute-start(bf16[2,128,768]{2,1,0:T(8,128)(2,1)S(1)} %constant_dynamic-update-slice_fusion.10.refs_9_), channel_id=1, source_target_pairs={{0,2},{1,3},{2,0},{3,1},{4,6},{5,7},{6,4},{7,5},{8,10},{9,11},{10,... | collective-permute-start | bytes 1179656 | tf_op jit(solution)/shard_map/cond/branch_2_fun/ppermute | solution.py:28
  28.7 0.0 collective-permute-done.29.refs_10_
  28.7 0.1 collective-permute-done.30.refs_11_
  28.7 0.7 %collective-permute-start.31 = (bf16[2,128,768]{2,1,0:T(8,128)(2,1)S(1)}, bf16[2,128,768]{2,1,0:T(8,128)(2,1)S(1)}, u32[]{:S(2)}, u32[]{:S(2)}) collective-permute-start(bf16[2,128,768]{2,1,0:T(8,128)(2,1)S(1)} %collective-permute-done.29.refs_10_), channel_id=1, source_target_pairs={{0,1},{1,0},{2,3},{3,2},{4,5},{5,4},{6,7},{7,6},{8,9},{9,8},{10,11... | collective-permute-start | bytes 1179656 | tf_op jit(solution)/shard_map/cond/branch_2_fun/ppermute | solution.py:28
  29.4 0.0 collective-permute-done.32.refs_8_
  29.4 5.8 %branch_2_fun.5 = (f32[2048,256]{1,0:T(8,128)S(1)}, f32[2,32,128]{2,1,0:T(8,128)S(1)}) custom-call(f32[64,768]{1,0:T(8,128)S(1)} %copy-done.7, f32[64,768]{1,0:T(8,128)S(1)} %copy-done.3, f32[2048,256]{1,0:T(8,128)S(1)} %branch_2_fun.4.refs_2_, s32[4,1024]{1,0:T(4,128)S(1)} %copy-done.16, s32[2,8]{1,0:T(2,128)S(1)} %copy-done.12, ...), custom_call_target="tpu_custom_call" | custom-call | flops 3221225472 | bytes 1769472 | tf_op jit(solution)/shard_map/cond/branch_2_fun/pallas_call | solution.py:251
  35.3 2.5 %collective-permute-done.28.refs_5_ = bf16[2,128,768]{2,1,0:T(8,128)(2,1)S(1)} collective-permute-done((bf16[2,128,768]{2,1,0:T(8,128)(2,1)S(1)}, bf16[2,128,768]{2,1,0:T(8,128)(2,1)S(1)}, u32[]{:S(2)}, u32[]{:S(2)}) %collective-permute-start.28) | collective-permute-done | bytes 393248 | tf_op jit(solution)/shard_map/cond/branch_2_fun/ppermute | solution.py:28
  37.7 1.3 %collective-permute-start.33 = (bf16[2,128,768]{2,1,0:T(8,128)(2,1)S(1)}, bf16[2,128,768]{2,1,0:T(8,128)(2,1)S(1)}, u32[]{:S(2)}, u32[]{:S(2)}) collective-permute-start(bf16[2,128,768]{2,1,0:T(8,128)(2,1)S(1)} %collective-permute-done.28.refs_5_), channel_id=1, source_target_pairs={{0,1},{1,0},{2,3},{3,2},{4,5},{5,4},{6,7},{7,6},{8,9},{9,8},{10,11... | collective-permute-start | bytes 1179656 | tf_op jit(solution)/shard_map/cond/branch_2_fun/ppermute | solution.py:28
  39.0 2.5 %branch_2_fun.6.refs_2_ = f32[2048,256]{1,0:T(8,128)S(1)} custom-call(f32[64,768]{1,0:T(8,128)S(1)} %copy-done.7, f32[64,768]{1,0:T(8,128)S(1)} %copy-done.3, f32[2048,256]{1,0:T(8,128)S(1)} %get-tuple-element.205.refs_2_, bf16[1,32,1536]{2,1,0:T(8,128)(2,1)S(1)} %get-tuple-element.201.refs_7_.refs_3_, ...), custom_call_target="tpu_custom_call" | custom-call | flops 1610612736 | bytes 884736 | tf_op jit(solution)/shard_map/cond/branch_2_fun/pallas_call | solution.py:251
  41.6 2.2 %branch_2_fun.7 = bf16[2,32,8192]{2,1,0:T(8,128)(2,1)S(1)} custom-call(f32[64,768]{1,0:T(8,128)S(1)} %copy-done.7, f32[64,768]{1,0:T(8,128)S(1)} %copy-done.3, f32[2048,256]{1,0:T(8,128)S(1)} %branch_2_fun.6.refs_2_, f32[2,32,128]{2,1,0:T(8,128)S(1)} %get-tuple-element.209.refs_3_, s32[2,8]{1,0:T(2,128)S(1)} %copy-done.12, ...), custom_call_target="tpu_custom_call" | custom-call | flops 805306368 | bytes 442368 | tf_op jit(solution)/shard_map/cond/branch_2_fun/pallas_call | solution.py:251
  43.9 0.0 copy-start.9
  44.0 1.0 %copy-done.9 = bf16[2,32,8192]{2,1,0:T(8,128)(2,1)} copy-done((bf16[2,32,8192]{2,1,0:T(8,128)(2,1)}, bf16[2,32,8192]{2,1,0:T(8,128)(2,1)S(1)}, u32[]{:S(2)}) %copy-start.9) | copy-done | bytes 1048600
  (19 shorter events, 0.2 us)
Async XLA Ops:
  0.0 1.0 %copy-start = (bf16[1,128,1536]{2,1,0:T(8,128)(2,1)S(1)}, bf16[1,128,1536]{2,1,0:T(8,128)(2,1)}, u32[]{:S(2)}) copy-start(bf16[1,128,1536]{2,1,0:T(8,128)(2,1)} %spectra_ref.1) | copy-start | bytes 1179652
  3.3 15.2 %copy-start.3 = (f32[64,768]{1,0:T(8,128)S(1)}, f32[64,768]{1,0:T(8,128)}, u32[]{:S(2)}) copy-start(f32[64,768]{1,0:T(8,128)} %get-tuple-element.179.refs_1_) | copy-start | bytes 589828 | tf_op jit(solution)/shard_map/cond
  3.3 15.2 %copy-start.7 = (f32[64,768]{1,0:T(8,128)S(1)}, f32[64,768]{1,0:T(8,128)}, u32[]{:S(2)}) copy-start(f32[64,768]{1,0:T(8,128)} %get-tuple-element.178.refs_0_) | copy-start | bytes 589828 | tf_op jit(solution)/shard_map/cond
  3.3 13.8 %collective-permute-start.26 = (bf16[1,128,768]{2,1,0:T(8,128)(2,1)S(1)}, bf16[1,128,768]{2,1,0:T(8,128)(2,1)S(1)}, u32[]{:S(2)}, u32[]{:S(2)}) collective-permute-start(bf16[1,128,768]{2,1,0:T(8,128)(2,1)S(1)} %get-tuple-element.187), channel_id=1, source_target_pairs={{0,20},{4,16},{8,28},{12,24},{16,4},{20,0},{24,12},{28,8},{1,21},{... | collective-permute-start | bytes 589832 | tf_op jit(solution)/shard_map/cond/branch_2_fun/ppermute | solution.py:28
  7.5 9.6 %collective-permute-start.25 = (bf16[1,128,768]{2,1,0:T(8,128)(2,1)S(1)}, bf16[1,128,768]{2,1,0:T(8,128)(2,1)S(1)}, u32[]{:S(2)}, u32[]{:S(2)}) collective-permute-start(bf16[1,128,768]{2,1,0:T(8,128)(2,1)S(1)} %get-tuple-element.187), channel_id=1, source_target_pairs={{0,8},{4,12},{8,0},{12,4},{16,24},{20,28},{24,16},{28,20},{1,9},{5... | collective-permute-start | bytes 589832 | tf_op jit(solution)/shard_map/cond/branch_2_fun/ppermute | solution.py:28
  8.8 5.2 %collective-permute-start.22 = (bf16[1,64,1536]{2,1,0:T(8,128)(2,1)S(1)}, bf16[1,64,1536]{2,1,0:T(8,128)(2,1)S(1)}, u32[]{:S(2)}, u32[]{:S(2)}) collective-permute-start(bf16[1,64,1536]{2,1,0:T(8,128)(2,1)S(1)} %get-tuple-element.268), channel_id=1, source_target_pairs={{0,2},{1,3},{2,0},{3,1},{4,6},{5,7},{6,4},{7,5},{8,10},{9,11},{10,... | collective-permute-start | bytes 589832 | tf_op jit(solution)/shard_map/cond/branch_2_fun/ppermute | solution.py:28
  14.1 12.1 %collective-permute-start.24 = (bf16[1,128,768]{2,1,0:T(8,128)(2,1)S(1)}, bf16[1,128,768]{2,1,0:T(8,128)(2,1)S(1)}, u32[]{:S(2)}, u32[]{:S(2)}) collective-permute-start(bf16[1,128,768]{2,1,0:T(8,128)(2,1)S(1)} %get-tuple-element.184), channel_id=1, source_target_pairs={{0,20},{4,16},{8,28},{12,24},{16,4},{20,0},{24,12},{28,8},{1,21},{... | collective-permute-start | bytes 589832 | tf_op jit(solution)/shard_map/cond/branch_2_fun/ppermute | solution.py:28
  14.2 12.0 %collective-permute-start.23 = (bf16[1,128,768]{2,1,0:T(8,128)(2,1)S(1)}, bf16[1,128,768]{2,1,0:T(8,128)(2,1)S(1)}, u32[]{:S(2)}, u32[]{:S(2)}) collective-permute-start(bf16[1,128,768]{2,1,0:T(8,128)(2,1)S(1)} %get-tuple-element.184), channel_id=1, source_target_pairs={{0,8},{4,12},{8,0},{12,4},{16,24},{20,28},{24,16},{28,20},{1,9},{5... | collective-permute-start | bytes 589832 | tf_op jit(solution)/shard_map/cond/branch_2_fun/ppermute | solution.py:28
  14.7 3.8 %collective-permute-start.27 = (bf16[2,32,1536]{2,1,0:T(8,128)(2,1)S(1)}, bf16[2,32,1536]{2,1,0:T(8,128)(2,1)S(1)}, u32[]{:S(2)}, u32[]{:S(2)}) collective-permute-start(bf16[2,32,1536]{2,1,0:T(8,128)(2,1)S(1)} %pad_maximum_fusion.2), channel_id=1, source_target_pairs={{0,1},{1,0},{2,3},{3,2},{4,5},{5,4},{6,7},{7,6},{8,9},{9,8},{10,11... | collective-permute-start | bytes 589832 | tf_op jit(solution)/shard_map/cond/branch_2_fun/ppermute | solution.py:28
  17.2 12.2 %copy-start.12 = (s32[2,8]{1,0:T(2,128)S(1)}, s32[2,8]{1,0:T(2,128)}, u32[]{:S(2)}) copy-start(s32[2,8]{1,0:T(2,128)} %get-tuple-element.199.refs_4_) | copy-start | bytes 196 | tf_op jit(solution)/shard_map/cond
  17.2 12.2 %copy-start.16 = (s32[4,1024]{1,0:T(4,128)S(1)}, s32[4,1024]{1,0:T(4,128)}, u32[]{:S(2)}) copy-start(s32[4,1024]{1,0:T(4,128)} %get-tuple-element.198.refs_3_) | copy-start | bytes 49156 | tf_op jit(solution)/shard_map/cond
  17.2 11.5 %collective-permute-start.29 = (bf16[2,128,768]{2,1,0:T(8,128)(2,1)S(1)}, bf16[2,128,768]{2,1,0:T(8,128)(2,1)S(1)}, u32[]{:S(2)}, u32[]{:S(2)}) collective-permute-start(bf16[2,128,768]{2,1,0:T(8,128)(2,1)S(1)} %constant_dynamic-update-slice_fusion.8.refs_3_), channel_id=1, source_target_pairs={{0,2},{1,3},{2,0},{3,1},{4,6},{5,7},{6,4},{7,5},{8,10},{9,11},{10,... | collective-permute-start | bytes 1179656 | tf_op jit(solution)/shard_map/cond/branch_2_fun/ppermute | solution.py:28
  26.2 2.5 %collective-permute-start.30 = (bf16[2,128,768]{2,1,0:T(8,128)(2,1)S(1)}, bf16[2,128,768]{2,1,0:T(8,128)(2,1)S(1)}, u32[]{:S(2)}, u32[]{:S(2)}) collective-permute-start(bf16[2,128,768]{2,1,0:T(8,128)(2,1)S(1)} %constant_dynamic-update-slice_fusion.10.refs_9_), channel_id=1, source_target_pairs={{0,1},{1,0},{2,3},{3,2},{4,5},{5,4},{6,7},{7,6},{8,9},{9,8},{10,11... | collective-permute-start | bytes 1179656 | tf_op jit(solution)/shard_map/cond/branch_2_fun/ppermute | solution.py:28
  27.4 2.0 %collective-permute-start.32 = (bf16[2,128,768]{2,1,0:T(8,128)(2,1)S(1)}, bf16[2,128,768]{2,1,0:T(8,128)(2,1)S(1)}, u32[]{:S(2)}, u32[]{:S(2)}) collective-permute-start(bf16[2,128,768]{2,1,0:T(8,128)(2,1)S(1)} %constant_dynamic-update-slice_fusion.8.refs_3_), channel_id=1, source_target_pairs={{0,1},{1,0},{2,3},{3,2},{4,5},{5,4},{6,7},{7,6},{8,9},{9,8},{10,11... | collective-permute-start | bytes 1179656 | tf_op jit(solution)/shard_map/cond/branch_2_fun/ppermute | solution.py:28
  27.5 10.3 %collective-permute-start.28 = (bf16[2,128,768]{2,1,0:T(8,128)(2,1)S(1)}, bf16[2,128,768]{2,1,0:T(8,128)(2,1)S(1)}, u32[]{:S(2)}, u32[]{:S(2)}) collective-permute-start(bf16[2,128,768]{2,1,0:T(8,128)(2,1)S(1)} %constant_dynamic-update-slice_fusion.10.refs_9_), channel_id=1, source_target_pairs={{0,2},{1,3},{2,0},{3,1},{4,6},{5,7},{6,4},{7,5},{8,10},{9,11},{10,... | collective-permute-start | bytes 1179656 | tf_op jit(solution)/shard_map/cond/branch_2_fun/ppermute | solution.py:28
  28.7 9.0 %collective-permute-start.31 = (bf16[2,128,768]{2,1,0:T(8,128)(2,1)S(1)}, bf16[2,128,768]{2,1,0:T(8,128)(2,1)S(1)}, u32[]{:S(2)}, u32[]{:S(2)}) collective-permute-start(bf16[2,128,768]{2,1,0:T(8,128)(2,1)S(1)} %collective-permute-done.29.refs_10_), channel_id=1, source_target_pairs={{0,1},{1,0},{2,3},{3,2},{4,5},{5,4},{6,7},{7,6},{8,9},{9,8},{10,11... | collective-permute-start | bytes 1179656 | tf_op jit(solution)/shard_map/cond/branch_2_fun/ppermute | solution.py:28
  37.7 3.8 %collective-permute-start.33 = (bf16[2,128,768]{2,1,0:T(8,128)(2,1)S(1)}, bf16[2,128,768]{2,1,0:T(8,128)(2,1)S(1)}, u32[]{:S(2)}, u32[]{:S(2)}) collective-permute-start(bf16[2,128,768]{2,1,0:T(8,128)(2,1)S(1)} %collective-permute-done.28.refs_5_), channel_id=1, source_target_pairs={{0,1},{1,0},{2,3},{3,2},{4,5},{5,4},{6,7},{7,6},{8,9},{9,8},{10,11... | collective-permute-start | bytes 1179656 | tf_op jit(solution)/shard_map/cond/branch_2_fun/ppermute | solution.py:28
  43.9 1.0 %copy-start.9 = (bf16[2,32,8192]{2,1,0:T(8,128)(2,1)}, bf16[2,32,8192]{2,1,0:T(8,128)(2,1)S(1)}, u32[]{:S(2)}) copy-start(bf16[2,32,8192]{2,1,0:T(8,128)(2,1)S(1)} %get-tuple-element.335) | copy-start | bytes 3145732
